TPU v7x, 512 devices: a whole 4x8x8 slice. The times are simulated.
512 devices in a mesh: expert: 32 (over z_hi, y), replica: 16 (over x, z_lo, core).
Axes of the slice: x: 4, y: 8, z: 8 (z_hi: 4, z_lo: 2; z = z_hi * 2 + z_lo), core: 2. Of those that a mesh axis runs over, the one named last changes fastest.
Arguments:
- tokens: bfloat16 [16384, 3584], P(('expert', 'replica')), may hold values from -6 to 6
- cotangent: bfloat16 [16384, 3584], P(('expert', 'replica')), may hold values from -6 to 6
- assign: int32 [1024], P(('expert', 'replica')), may hold values from 0 to 3, as said below
- w_gate: bfloat16 [3584, 4096], P(None, 'expert'), may hold values from -0.09375 to 0.09375
- w_up: bfloat16 [3584, 4096], P(None, 'expert'), may hold values from -0.09375 to 0.09375
- w_down: bfloat16 [4096, 3584], P('expert'), may hold values from -0.1875 to 0.1875
Outputs:
- input_grad: bfloat16 [16384, 3584], P(('expert', 'replica'))
- grad_gate: float32 [3584, 4096], P('replica', 'expert')
- grad_up: float32 [3584, 4096], P('replica', 'expert')
- grad_down: float32 [4096, 3584], P('expert', 'replica')
Inputs may be any that keep to these rules, and one draw needn't show every extreme that they name: `assign`: block k has replica index (k // 2) % 16. The two blocks 2i and 2i+1 go to two different experts. Let L(e, r) count the blocks of replica index r that go to expert e: for every r one expert has L = 32, every L(e, r) is at least 10, and L(e, r) + L(e, r + 8) is at most 43; both bounds are reached for every r.
All inputs are finite; a program needn't handle non-finite values.
Results may differ from a plain program's by a relative error of at most 0.022.
Values may be sent and summed in bfloat16 or wider, within the bound.
A program may use at most 64 MiB of HBM per device.

v0:
```python
import math

import jax
import jax.numpy as jnp
from jax import lax
from jax.sharding import PartitionSpec as P

E_WIN = 4


def backprop(blocks_x, blocks_dy, w_gate, w_up, w_down):
    row_count = blocks_x.shape[0] * blocks_x.shape[1]
    features = blocks_x.shape[2]
    flat_x = blocks_x.reshape(row_count, features)
    flat_dy = blocks_dy.reshape(row_count, features)
    gate_pre = jnp.dot(flat_x, w_gate, preferred_element_type=jnp.float32)
    up_pre = jnp.dot(flat_x, w_up, preferred_element_type=jnp.float32)
    sig_gate = jax.nn.sigmoid(gate_pre)
    silu_gate = gate_pre * sig_gate
    hidden = (silu_gate * up_pre).astype(jnp.bfloat16)
    d_hidden = lax.dot_general(
        flat_dy, w_down, (((1,), (1,)), ((), ())), preferred_element_type=jnp.float32
    )
    by_rows = (((0,), (0,)), ((), ()))
    by_cols = (((1,), (1,)), ((), ()))
    d_up = (d_hidden * silu_gate).astype(jnp.bfloat16)
    d_gate = (d_hidden * up_pre * sig_gate * (1.0 + gate_pre * (1.0 - sig_gate))).astype(
        jnp.bfloat16
    )
    partial_value = lax.dot_general(d_gate, w_gate, by_cols, preferred_element_type=jnp.float32)
    partial_value = partial_value + lax.dot_general(
        d_up, w_up, by_cols, preferred_element_type=jnp.float32
    )
    grad_gate = lax.dot_general(flat_x, d_gate, by_rows, preferred_element_type=jnp.float32)
    grad_up = lax.dot_general(flat_x, d_up, by_rows, preferred_element_type=jnp.float32)
    grad_down = lax.dot_general(flat_dy, hidden, by_rows, preferred_element_type=jnp.float32)
    gate_sum, up_sum, down_sum = (
        lax.psum_scatter(
            grad_gate.astype(jnp.bfloat16), "replica", scatter_dimension=0, tiled=True
        ).astype(jnp.float32),
        lax.psum_scatter(
            grad_up.astype(jnp.bfloat16), "replica", scatter_dimension=0, tiled=True
        ).astype(jnp.float32),
        lax.psum_scatter(
            grad_down.astype(jnp.bfloat16), "replica", scatter_dimension=0, tiled=True
        ).astype(jnp.float32),
    )
    partial_value = partial_value.astype(jnp.bfloat16).reshape(blocks_x.shape)
    return (partial_value, gate_sum, up_sum, down_sum)


def shards(tokens, cotangent, assign, w_gate, w_up, w_down):
    experts = lax.axis_size("expert")
    replicas = lax.axis_size("replica")
    sharing = experts // E_WIN
    block_rows = tokens.shape[0] // 2
    features = tokens.shape[1]
    own_x = tokens.reshape(2, block_rows, features)
    own_dy = cotangent.reshape(2, block_rows, features)
    group_of = jnp.arange(experts, dtype=jnp.int32) // sharing
    to_first = (assign[0] == group_of)[:, None, None]
    to_second = (assign[1] == group_of)[:, None, None]
    blank_rows = jnp.zeros((experts, block_rows, features), jnp.bfloat16)
    send_x = jnp.where(to_first, own_x[0], jnp.where(to_second, own_x[1], blank_rows))
    send_dy = jnp.where(to_first, own_dy[0], jnp.where(to_second, own_dy[1], blank_rows))
    send_flags = jnp.logical_or(to_first, to_second).reshape(experts).astype(jnp.bfloat16)
    recv_x, recv_dy, live_flags = (
        lax.all_to_all(send_x, "expert", split_axis=0, concat_axis=0, tiled=True),
        lax.all_to_all(send_dy, "expert", split_axis=0, concat_axis=0, tiled=True),
        lax.all_to_all(send_flags, "expert", split_axis=0, concat_axis=0, tiled=True),
    )
    result_back, gate_sum, up_sum, down_sum = backprop(recv_x, recv_dy, w_gate, w_up, w_down)
    returned = lax.all_to_all(result_back, "expert", split_axis=0, concat_axis=0, tiled=True)
    own_parts = jnp.take(
        returned.reshape(E_WIN, sharing, block_rows, features), assign, axis=0, mode="clip"
    )
    input_grad = (
        jnp.sum(own_parts.astype(jnp.float32), axis=1)
        .astype(jnp.bfloat16)
        .reshape(2 * block_rows, features)
    )
    grad_scale = 1.0 / math.sqrt(experts * replicas * block_rows // 2)
    return (
        input_grad,
        gate_sum * grad_scale,
        up_sum * grad_scale,
        jnp.transpose(down_sum * grad_scale),
    )


def solution(mesh):
    placed = (
        P(("expert", "replica"), None),
        P(("expert", "replica"), None),
        P(("expert", "replica")),
        P(None, "expert"),
        P(None, "expert"),
        P("expert", None),
    )
    return jax.shard_map(
        shards,
        mesh=mesh,
        in_specs=placed,
        out_specs=(
            P(("expert", "replica"), None),
            P("replica", "expert"),
            P("replica", "expert"),
            P("expert", "replica"),
        ),
        check_vma=False,
    )
```

profile of v0, /device:TPU:6, one launch (start us, length us, event | category | flops | bytes accessed | tf_op | source)
XLA Modules:
  0.0 534.8 jit_solution(12354311271712948217)
XLA Ops:
  7.2 0.0 copy-start
  7.2 1.3 fusion.6
  8.5 1.3 broadcast_compare_fusion
  9.8 1.1 fusion.4
  10.9 2.4 select_select_fusion.1
  13.4 102.5 %all_to_all.15 = bf16[32,16,3584]{2,1,0:T(8,128)(2,1)} all-to-all(bf16[32,16,3584]{2,1,0:T(8,128)(2,1)S(1)} %get-tuple-element.11), channel_id=1, replica_groups=mesh['expert'=32,'replica'=16] {'expert'}, dimensions={0} | all-to-all | bytes 7340032 | tf_op jit(solution)/shard_map/all_to_all | solution.py:68
  115.9 10.2 %all-to-all-start = ((bf16[32,16,3584]{2,1,0:T(8,128)(2,1)}), bf16[32,16,3584]{2,1,0:T(8,128)(2,1)}, u32[]{:S(2)}, u32[]{:S(2)}) async-start(bf16[32,16,3584]{2,1,0:T(8,128)(2,1)} %get-tuple-element.10), calls=%async_computation | async-start | bytes 7340032 | tf_op jit(solution)/shard_map/all_to_all | solution.py:69
  126.1 3.3 fusion.8
  129.4 0.0 copy-done.2
  129.4 1.1 fusion.7
  130.5 103.3 %all-to-all-done = bf16[32,16,3584]{2,1,0:T(8,128)(2,1)} async-done(((bf16[32,16,3584]{2,1,0:T(8,128)(2,1)}), bf16[32,16,3584]{2,1,0:T(8,128)(2,1)}, u32[]{:S(2)}, u32[]{:S(2)}) %all-to-all-start) | async-done | bytes 3670048 | tf_op jit(solution)/shard_map/all_to_all | solution.py:69
  233.9 3.1 multiply_convert_fusion.1
  237.0 1.1 fusion.9
  238.1 3.0 add_convert_fusion
  241.1 18.9 %all-to-all-start.2 = ((bf16[32,16,3584]{2,1,0:T(8,128)(2,1)}), bf16[32,16,3584]{2,1,0:T(8,128)(2,1)}, u32[]{:S(2)}, u32[]{:S(2)}) async-start(bf16[32,16,3584]{2,1,0:T(8,128)(2,1)} %bitcast.28), calls=%async_computation.2 | async-start | bytes 7340032 | tf_op jit(solution)/shard_map/all_to_all | solution.py:73
  260.0 0.0 reduce-scatter.8.cloned.1.call-start
  260.1 4.2 convolution_convert_fusion
  264.3 0.0 reduce-scatter.8.cloned.1.call-update
  264.3 0.0 reduce-scatter.6.cloned.1.call-start
  264.4 4.2 convolution_convert_fusion.1
  268.5 0.0 reduce-scatter.6.cloned.1.call-update
  268.5 0.0 reduce-scatter.4.cloned.1.call-start
  268.6 4.1 convolution_convert_fusion.2
  272.7 0.0 reduce-scatter.4.cloned.1.call-update
  272.8 97.7 %reduce-scatter.8.cloned.1.call-done = bf16[224,128]{1,0:T(8,128)(2,1)} async-done(((bf16[3584,128]{1,0:T(8,128)(2,1)}), bf16[224,128]{1,0:T(8,128)(2,1)}) %reduce-scatter.8.cloned.1.call-update) | async-done | bytes 57360 | tf_op jit(solution)/shard_map/reduce_scatter | solution.py:44
  370.5 1.5 multiply_bitcast_fusion
  371.9 83.3 %reduce-scatter.6.cloned.1.call-done = bf16[224,128]{1,0:T(8,128)(2,1)} async-done(((bf16[3584,128]{1,0:T(8,128)(2,1)}), bf16[224,128]{1,0:T(8,128)(2,1)}) %reduce-scatter.6.cloned.1.call-update) | async-done | bytes 57360 | tf_op jit(solution)/shard_map/reduce_scatter | solution.py:41
  455.2 1.5 convert_multiply_fusion
  456.7 66.4 %reduce-scatter.4.cloned.1.call-done = bf16[224,128]{1,0:T(8,128)(2,1)} async-done(((bf16[3584,128]{1,0:T(8,128)(2,1)}), bf16[224,128]{1,0:T(8,128)(2,1)}) %reduce-scatter.4.cloned.1.call-update) | async-done | bytes 57360 | tf_op jit(solution)/shard_map/reduce_scatter | solution.py:38
  523.1 1.5 convert_multiply_fusion.1
  524.5 2.7 gather_fusion
  527.2 1.0 reduce_sum.12
  (10 shorter events, 0.0 us)
Async XLA Ops:
  7.2 118.9 %copy-start = (bf16[3584,128]{1,0:T(8,128)(2,1)S(1)}, bf16[3584,128]{1,0:T(8,128)(2,1)}, u32[]{:S(2)}) copy-start(bf16[3584,128]{1,0:T(8,128)(2,1)} %param.9) | copy-start | bytes 2752516
  115.9 118.0 %all-to-all-start = ((bf16[32,16,3584]{2,1,0:T(8,128)(2,1)}), bf16[32,16,3584]{2,1,0:T(8,128)(2,1)}, u32[]{:S(2)}, u32[]{:S(2)}) async-start(bf16[32,16,3584]{2,1,0:T(8,128)(2,1)} %get-tuple-element.10), calls=%async_computation | async-start | bytes 7340032 | tf_op jit(solution)/shard_map/all_to_all | solution.py:69
  126.0 3.3 copy-start.1
  126.0 3.4 copy-start.2
  126.1 107.8 %copy-start.4 = (bf16[128,3584]{1,0:T(8,128)(2,1)S(1)}, bf16[128,3584]{1,0:T(8,128)(2,1)}, u32[]{:S(2)}) copy-start(bf16[128,3584]{1,0:T(8,128)(2,1)} %param.11) | copy-start | bytes 2752516
  241.1 283.4 %all-to-all-start.2 = ((bf16[32,16,3584]{2,1,0:T(8,128)(2,1)}), bf16[32,16,3584]{2,1,0:T(8,128)(2,1)}, u32[]{:S(2)}, u32[]{:S(2)}) async-start(bf16[32,16,3584]{2,1,0:T(8,128)(2,1)} %bitcast.28), calls=%async_computation.2 | async-start | bytes 7340032 | tf_op jit(solution)/shard_map/all_to_all | solution.py:73
  260.0 110.4 %reduce-scatter.8.cloned.1.call-start = ((), (), s32[]{:S(2)}) async-start(), calls=%async_computation.8 | async-start | bytes 974848 | tf_op jit(solution)/shard_map/reduce_scatter | solution.py:44
  264.3 190.9 %reduce-scatter.6.cloned.1.call-start = ((), (), s32[]{:S(2)}) async-start(), calls=%async_computation.7 | async-start | bytes 974848 | tf_op jit(solution)/shard_map/reduce_scatter | solution.py:41
  268.5 4.2 copy-start.3
  268.5 254.5 %reduce-scatter.4.cloned.1.call-start = ((), (), s32[]{:S(2)}) async-start(), calls=%async_computation.6 | async-start | bytes 974848 | tf_op jit(solution)/shard_map/reduce_scatter | solution.py:38
Sparse Core Ops, SparseCore 0:
  264.4 106.0 reduce-scatter.7
  373.5 81.6 reduce-scatter.5
  458.0 64.9 reduce-scatter.3
where the time goes:
time: 542 us; the launch traced here: 535 us
  waiting for transfers between devices  351 us (65%)
  blocking collectives  103 us (19%)
  starting transfers between devices  29.2 us (5%)
  matrix products  24.1 us (4%)
  between operations  13.9 us (3%)
  other arithmetic  9.14 us (2%)
    all_to_all x1, waiting for transfers between devices, shards(): lax.all_to_all(send_dy, 'expert', split_axis=0, concat_axis=0, tiled=True)  103 us
    all_to_all x1, blocking collectives, shards(): lax.all_to_all(send_x, 'expert', split_axis=0, concat_axis=0, tiled=True)  103 us
    reduce_scatter x1, waiting for transfers between devices, backprop(): lax.psum_scatter(grad_down.astype(jnp.bfloat16), 'replica', scatter_dimen...  97.7 us
    reduce_scatter x1, waiting for transfers between devices, backprop(): lax.psum_scatter(grad_up.astype(jnp.bfloat16), 'replica', scatter_dimensi...  83.3 us
    reduce_scatter x1, waiting for transfers between devices, backprop(): lax.psum_scatter(grad_gate.astype(jnp.bfloat16), 'replica', scatter_dimen...  66.4 us
    all_to_all x1, starting transfers between devices, shards(): lax.all_to_all(result_back, 'expert', split_axis=0, concat_axis=0, tiled=...  18.9 us
  transfers between devices with their start and end apart: 5, of which 4 were waited for; matrix products, arithmetic and copies ran while one was open for 4% of the time, Pallas kernels for 0%

commit v1 on v0

v1 whole, which is shorter than its diff:
```python
import functools
import math

import jax
import jax.numpy as jnp
from jax import lax
from jax.experimental import pallas as pl
from jax.experimental.pallas import tpu as pltpu
from jax.sharding import PartitionSpec as P

E_WIN = 4
NY = 8
NX = 4
BLK = 16
D = 3584
SLICE = 128
ROWS = 224
STEP = 512
MESH = pl.DeviceIdType.MESH
LEAN = (1, -1, 1, -1)


def place():
    ex = lax.axis_index("expert")
    rp = lax.axis_index("replica")
    z, y = lax.div(ex, NY), lax.rem(ex, NY)
    q, core = lax.div(rp, 2), lax.rem(rp, 2)
    x, zl = lax.div(q, 2), lax.rem(q, 2)

    def at_z(i):
        return (lax.rem(z + i, E_WIN) * NY + y, rp)

    def at_y(d):
        return (z * NY + lax.rem(y + NY + d, NY), rp)

    def at_x(i):
        return (ex, lax.rem(x + i, NX) * 4 + zl * 2 + core)

    pair = (ex, x * 4 + (1 - zl) * 2 + core)
    sibling = (ex, q * 2 + 1 - core)
    return z, x, zl, q, core, at_z, at_y, at_x, pair, sibling


def greet(peers):
    barrier = pltpu.get_barrier_semaphore()
    for peer in peers:
        pl.semaphore_signal(barrier, inc=1, device_id=peer, device_id_type=MESH)
    pl.semaphore_wait(barrier, len(peers))


def remote(src, dst, send_sem, recv_sem, peer):
    return pltpu.make_async_remote_copy(
        src_ref=src, dst_ref=dst, send_sem=send_sem, recv_sem=recv_sem, device_id=peer, device_id_type=MESH
    )


def dispatch_kernel(send, wg, wu, wd, rows, go, uo, do, zs, zr, ys, yr, ls, ws, wr):
    z, x, zl, q, core, at_z, at_y, at_x, pair, sibling = place()
    greet([at_z(i) for i in (1, 2, 3)] + [at_y(1), at_y(-1), at_y(4)] + [at_x(i) for i in (1, 2, 3)] + [pair, sibling])
    half = pl.ds(pl.multiple_of(core * (D // 2), 128), D // 2)

    def weights(srcs, dsts, base, peer):
        return [remote(s, d, ws.at[base + n], wr.at[base + n], peer) for n, (s, d) in enumerate(zip(srcs, dsts))]

    def start(copies):
        for c in copies:
            c.start()

    one = [go.at[core, q], uo.at[core, q], do.at[q, :, half]]
    stage1 = weights([wg.at[core, q], wu.at[core, q], wd.at[q, :, half]], one, 0, at_y(4))
    stage2 = weights(one, one, 3, pair)
    two = pl.ds(2 * x, 2)
    both = [go.at[core, two], uo.at[core, two], do.at[two, :, half]]
    stage3 = [weights(both, both, 6 + 3 * (i - 1), at_x(i)) for i in (1, 2, 3)]
    every = [go.at[core], uo.at[core], do.at[:, :, half]]
    stage4 = weights(every, every, 15, sibling)

    by_z = {
        4 - i: remote(send.at[lax.rem(z + i, E_WIN)], rows.at[4 - i, 0], zs.at[i - 1], zr.at[3 - i], at_z(i))
        for i in (1, 2, 3)
    }

    def by_y(j):
        src = send.at[z] if j == 0 else rows.at[j, 0]
        s = LEAN[j]
        return [
            remote(src, rows.at[j, 1], ys.at[j, 0], yr.at[j, 0], at_y(s)),
            remote(src, rows.at[j, 2], ys.at[j, 1], yr.at[j, 1], at_y(-s)),
            remote(rows.at[j, 1], rows.at[j, 3], ys.at[j, 2], yr.at[j, 2], at_y(s)),
        ]

    along_y = [by_y(j) for j in range(E_WIN)]
    own = pltpu.make_async_copy(send.at[z], rows.at[0, 0], ls)

    start(stage1)
    for j in (1, 3, 2):
        by_z[j].start()
    start(along_y[0][:2])
    own.start()
    along_y[0][0].wait_recv()
    along_y[0][2].start()
    for c in stage1:
        c.wait_recv()
    start(stage2)
    for j in (1, 3):
        by_z[j].wait_recv()
        start(along_y[j][:2])
    for c in stage2:
        c.wait_recv()
    for group in stage3:
        start(group)
    for j in (1, 3):
        along_y[j][0].wait_recv()
        along_y[j][2].start()
    by_z[2].wait_recv()
    start(along_y[2][:2])
    along_y[2][0].wait_recv()
    along_y[2][2].start()
    for group in stage3:
        for c in group:
            c.wait_recv()
    start(stage4)
    for j in range(E_WIN):
        along_y[j][1].wait_recv()
        along_y[j][2].wait_recv()
    for c in stage4:
        c.wait_recv()
    own.wait()
    for j in (1, 2, 3):
        by_z[j].wait_send()
    for group in along_y + stage3 + [stage1, stage2, stage4]:
        for c in group:
            c.wait_send()


def dispatch(send, wg, wu, wd):
    out = jax.ShapeDtypeStruct
    bf = jnp.bfloat16
    dma = pltpu.SemaphoreType.DMA
    anywhere = pl.BlockSpec(memory_space=pl.ANY)
    rows, go, uo, do = pl.pallas_call(
        dispatch_kernel,
        out_shape=(
            out((E_WIN, 4, BLK, 2 * D), bf),
            out((2, 8, ROWS, SLICE), bf),
            out((2, 8, ROWS, SLICE), bf),
            out((8, BLK, D), bf),
        ),
        in_specs=[anywhere] * 4,
        out_specs=[anywhere] * 4,
        scratch_shapes=[dma((3,)), dma((3,)), dma((4, 3)), dma((4, 3)), dma, dma((18,)), dma((18,))],
        compiler_params=pltpu.CompilerParams(collective_id=0, has_side_effects=True),
        name="dispatch",
    )(send, wg.reshape(2, 8, ROWS, SLICE), wu.reshape(2, 8, ROWS, SLICE), wd.reshape(8, BLK, D))
    return rows.reshape(16 * BLK, 2 * D), go.reshape(D, SLICE), uo.reshape(D, SLICE), do.reshape(SLICE, D)


def expert_kernel(x, dy, wg, go, wu, uo, wd, do, px, dw, pre, dh, dcat, hid):
    phase, step = pl.program_id(0), pl.program_id(1)
    by_cols = (((1,), (1,)), ((), ()))
    by_rows = (((0,), (0,)), ((), ()))
    f32 = jnp.float32

    @pl.when(phase == 0)
    def _():
        @pl.when(step == 0)
        def _():
            pre[...] = jnp.zeros_like(pre)
            dh[...] = jnp.zeros_like(dh)

        w = jnp.concatenate([wg[...], go[...], wu[...], uo[...]], axis=1)
        pre[...] += jnp.dot(x[...], w, preferred_element_type=f32)
        down = jnp.concatenate([wd[...], do[...]], axis=0)
        dh[...] += lax.dot_general(dy[...], down, by_cols, preferred_element_type=f32)

    @pl.when(phase == 1)
    def _():
        @pl.when(step == 0)
        def _():
            gate, up = pre[:, : 2 * SLICE], pre[:, 2 * SLICE :]
            grad = dh[...]
            sig = jax.nn.sigmoid(gate)
            silu = gate * sig
            hid[...] = (silu * up).astype(jnp.bfloat16)
            dcat[:, 2 * SLICE :] = (grad * silu).astype(jnp.bfloat16)
            dcat[:, : 2 * SLICE] = (grad * up * sig * (1.0 + gate * (1.0 - sig))).astype(jnp.bfloat16)

        w = jnp.concatenate([wg[...], go[...], wu[...], uo[...]], axis=1)
        px[...] = lax.dot_general(dcat[...], w, by_cols, preferred_element_type=f32).astype(jnp.bfloat16)
        both = lax.dot_general(x[...], dcat[...], by_rows, preferred_element_type=f32).astype(jnp.bfloat16)
        dw[0] = both[:, : 2 * SLICE]
        dw[1] = both[:, 2 * SLICE :]
        dw[2] = lax.dot_general(dy[...], hid[...], by_rows, preferred_element_type=f32).astype(jnp.bfloat16)


def expert(rows, wg, go, wu, uo, wd, do):
    n = rows.shape[0]
    steps = D // STEP
    bf = jnp.bfloat16
    tall = pl.BlockSpec((STEP, SLICE), lambda p, k: (k, 0))
    wide = pl.BlockSpec((SLICE, STEP), lambda p, k: (0, k))
    return pl.pallas_call(
        expert_kernel,
        grid=(2, steps),
        out_shape=(jax.ShapeDtypeStruct((n, D), bf), jax.ShapeDtypeStruct((3, D, 2 * SLICE), bf)),
        in_specs=[
            pl.BlockSpec((n, STEP), lambda p, k: (0, k)),
            pl.BlockSpec((n, STEP), lambda p, k: (0, k + steps)),
            tall, tall, tall, tall, wide, wide,
        ],
        out_specs=(
            pl.BlockSpec((n, STEP), lambda p, k: (0, k * p)),
            pl.BlockSpec((3, STEP, 2 * SLICE), lambda p, k: (0, k * p, 0)),
        ),
        scratch_shapes=[
            pltpu.VMEM((n, 4 * SLICE), jnp.float32),
            pltpu.VMEM((n, 2 * SLICE), jnp.float32),
            pltpu.VMEM((n, 4 * SLICE), bf),
            pltpu.VMEM((n, 2 * SLICE), bf),
        ],
        compiler_params=pltpu.CompilerParams(vmem_limit_bytes=40 * 2**20),
        cost_estimate=pl.CostEstimate(flops=16 * n * D * 2 * SLICE, bytes_accessed=30 * 2**20, transcendentals=0),
        name="expert",
    )(rows, rows, wg, go, wu, uo, wd, do)


def combine_kernel(scale, px, dw, ret, out, parts, sums, mine, theirs, from_x, s2, from_z, s3, from_y,
                   ls, ps, pr, zs, zr, c_s, c_r, xs, xr, gs, gr, ys, yr):
    z, x, zl, q, core, at_z, at_y, at_x, pair, sibling = place()
    f32, bf = jnp.float32, jnp.bfloat16
    greet([at_z(i) for i in (1, 2, 3)] + [at_y(d) for d in (1, -1, 2, -2, 4)] + [at_x(i) for i in (1, 2, 3)] + [pair, sibling])

    to_core = [remote(dw.at[k, :, 1 - core], theirs.at[k], c_s.at[k], c_r.at[k], sibling) for k in range(3)]
    keep = [pltpu.make_async_copy(dw.at[k, :, core], mine.at[k], ls.at[k]) for k in range(3)]
    own = [pltpu.make_async_copy(px.at[j, 0], parts.at[j, 0], ls.at[3 + j]) for j in range(E_WIN)]
    back = [
        [
            remote(px.at[j, o], parts.at[j, o], ps.at[j, o - 1], pr.at[j, o - 1], at_y(d * LEAN[j]))
            for o, d in ((1, -1), (2, 1), (3, -2))
        ]
        for j in range(E_WIN)
    ]
    to_x = [
        [
            remote(mine.at[k, pl.ds(2 * lax.rem(x + i, NX), 2)], from_x.at[k, i - 1], xs.at[k, i - 1], xr.at[k, i - 1], at_x(i))
            for i in (1, 2, 3)
        ]
        for k in range(3)
    ]
    to_pair = [remote(s2.at[k, 1 - zl], from_z.at[k], gs.at[k], gr.at[k], pair) for k in range(3)]
    to_y = [remote(s3.at[k, 1], from_y.at[k], ys.at[k], yr.at[k], at_y(4)) for k in range(3)]
    home = {j: remote(sums.at[j], ret.at[z], zs.at[j - 1], zr.at[j - 1], at_z(j)) for j in (1, 2, 3)}
    stay = pltpu.make_async_copy(sums.at[0], ret.at[z], ls.at[7])
    landing = {j: remote(sums.at[j], ret.at[lax.rem(z + 4 - j, E_WIN)], zs.at[j - 1], zr.at[j - 1], at_z(j)) for j in (1, 2, 3)}

    to_core[0].start()
    keep[0].start()
    for k in (1, 2):
        to_core[k].start()
        keep[k].start()
    for j in (2, 1, 3, 0):
        own[j].start()
        for c in back[j]:
            c.start()

    for k in range(3):
        keep[k].wait()
        to_core[k].wait_recv()

        @pl.loop(0, 8)
        def _(n):
            mine[k, n] = (mine[k, n].astype(f32) + theirs[k, n].astype(f32)).astype(bf)

        for c in to_x[k]:
            c.start()

    for j in (2, 1, 3, 0):
        own[j].wait()
        for c in back[j]:
            c.wait_recv()
        total = parts[j, 0].astype(f32)
        for o in (1, 2, 3):
            total += parts[j, o].astype(f32)
        sums[j] = total.astype(bf)
        if j:
            home[j].start()
        else:
            stay.start()

    for k in range(3):
        for c in to_x[k]:
            c.wait_recv()
        for n in range(2):
            total = mine[k, 2 * x + n].astype(f32)
            for i in range(3):
                total += from_x[k, i, n].astype(f32)
            s2[k, n] = total.astype(bf)
        to_pair[k].start()

    for k in range(3):
        to_pair[k].wait_recv()
        total = s2[k, zl].astype(f32) + from_z[k].astype(f32)
        s3[k, 0] = total[:, :SLICE].astype(bf)
        s3[k, 1] = total[:, SLICE:].astype(bf)
        to_y[k].start()

    for k in range(3):
        to_y[k].wait_recv()
        out[k] = (s3[k, 0].astype(f32) + from_y[k].astype(f32)) * scale

    stay.wait()
    for j in (1, 2, 3):
        landing[j].wait_recv()
        home[j].wait_send()
    for group in back + to_x + [to_core, to_pair, to_y]:
        for c in group:
            c.wait_send()


def combine(px, dw, scale):
    bf = jnp.bfloat16
    dma = pltpu.SemaphoreType.DMA
    anywhere = pl.BlockSpec(memory_space=pl.ANY)
    return pl.pallas_call(
        functools.partial(combine_kernel, scale),
        out_shape=(
            jax.ShapeDtypeStruct((E_WIN, BLK, D), bf),
            jax.ShapeDtypeStruct((3, ROWS, SLICE), jnp.float32),
        ),
        in_specs=[anywhere] * 2,
        out_specs=(anywhere, pl.BlockSpec(memory_space=pltpu.VMEM)),
        scratch_shapes=[
            pltpu.VMEM((E_WIN, 4, BLK, D), bf),
            pltpu.VMEM((E_WIN, BLK, D), bf),
            pltpu.VMEM((3, 8, ROWS, 2 * SLICE), bf),
            pltpu.VMEM((3, 8, ROWS, 2 * SLICE), bf),
            pltpu.VMEM((3, 3, 2, ROWS, 2 * SLICE), bf),
            pltpu.VMEM((3, 2, ROWS, 2 * SLICE), bf),
            pltpu.VMEM((3, ROWS, 2 * SLICE), bf),
            pltpu.VMEM((3, 2, ROWS, SLICE), bf),
            pltpu.VMEM((3, ROWS, SLICE), bf),
            dma((8,)),
            dma((4, 3)), dma((4, 3)),
            dma((3,)), dma((3,)),
            dma((3,)), dma((3,)),
            dma((3, 3)), dma((3, 3)),
            dma((3,)), dma((3,)),
            dma((3,)), dma((3,)),
        ],
        compiler_params=pltpu.CompilerParams(collective_id=1, has_side_effects=True, vmem_limit_bytes=40 * 2**20),
        name="combine",
    )(px.reshape(E_WIN, 4, BLK, D), dw.reshape(3, 8, 2, ROWS, 2 * SLICE))


def shards(tokens, cotangent, assign, w_gate, w_up, w_down):
    scale = 1.0 / math.sqrt(lax.axis_size("expert") * lax.axis_size("replica") * BLK // 2)
    own = jnp.concatenate([tokens, cotangent], axis=1).reshape(2, BLK, 2 * D)
    experts = jnp.arange(E_WIN, dtype=jnp.int32)
    first = (assign[0] == experts)[:, None, None]
    second = (assign[1] == experts)[:, None, None]
    send = jnp.where(first, own[0], jnp.where(second, own[1], jnp.zeros((), jnp.bfloat16)))
    rows, go, uo, do = dispatch(send, w_gate, w_up, w_down)
    px, dw = expert(rows, w_gate, go, w_up, uo, w_down, do)
    ret, grads = combine(px, dw, scale)
    picked = jnp.zeros((2, BLK, D), jnp.bfloat16)
    for e in range(E_WIN):
        picked = jnp.where((assign == e)[:, None, None], ret[e], picked)
    return picked.reshape(2 * BLK, D), grads[0], grads[1], jnp.transpose(grads[2])


def solution(mesh):
    placed = (
        P(("expert", "replica"), None),
        P(("expert", "replica"), None),
        P(("expert", "replica")),
        P(None, "expert"),
        P(None, "expert"),
        P("expert", None),
    )
    return jax.shard_map(
        shards,
        mesh=mesh,
        in_specs=placed,
        out_specs=(
            P(("expert", "replica"), None),
            P("replica", "expert"),
            P("replica", "expert"),
            P("expert", "replica"),
        ),
        check_vma=False,
    )
```

time: 542 us -> 138 us (0.25); the launches traced: 535 us -> 136 us
  waiting for transfers between devices: 351 us -> 0 us
  Pallas kernels: 0 us -> 119 us
  blocking collectives: 103 us -> 0 us
  starting transfers between devices: 29.2 us -> 0 us
  matrix products: 24.1 us -> 0 us
  between operations: 13.9 us -> 0.76 us
  local copies, waits for them, and re-layouts: 5.2 us -> 12.9 us
  other arithmetic: 9.14 us -> 3.23 us
    reduce_scatter x3 -> x0, waiting for transfers between devices: 247 us -> none  [the longest x1 97.7 us: backprop(): lax.psum_scatter(grad_down.astype(jnp.bfloat16), 'replica', scatter_dimen...]
    pallas_call x0 -> x3, Pallas kernels: none -> 119 us  [the longest x1 54.7 us: combine(): pl.pallas_call(functools.partial(combine_kernel, scale), out_shape=(jax.S...]
    all_to_all x2 -> x0, waiting for transfers between devices: 103 us -> none  [the longest x1 103 us: shards(): lax.all_to_all(send_dy, 'expert', split_axis=0, concat_axis=0, tiled=True)]
    all_to_all x1 -> x0, blocking collectives: 103 us -> none  [shards(): lax.all_to_all(send_x, 'expert', split_axis=0, concat_axis=0, tiled=True)]
    all_to_all x2 -> x0, starting transfers between devices: 29.1 us -> none  [the longest x1 18.9 us: shards(): lax.all_to_all(result_back, 'expert', split_axis=0, concat_axis=0, tiled=...]
    dot_general x8 -> x0, matrix products: 24.1 us -> none  [the longest x1 4.19 us: backprop(): lax.dot_general(flat_dy, hidden, by_rows, preferred_element_type=jnp.floa...]
    unnamed x10 -> x19, local copies, waits for them, and re-layouts: 0.06 us -> 9.11 us
  transfers between devices with their start and end apart: 5 -> 0, of which waited for: 4 -> 0; matrix products, arithmetic and copies ran while one was open for 4% -> 0% of each run, Pallas kernels for 0% -> 0%
where the time goes in v1:
time: 138 us; the launch traced here: 136 us
  Pallas kernels  119 us (86%)
  local copies, waits for them, and re-layouts  12.9 us (9%)
  other arithmetic  3.23 us (2%)
    pallas_call x1, Pallas kernels, combine(): pl.pallas_call(functools.partial(combine_kernel, scale), out_shape=(jax.S...  54.7 us
    pallas_call x1, Pallas kernels, dispatch(): pl.pallas_call(dispatch_kernel, out_shape=(out((E_WIN, 4, BLK, 2 * D), bf...  54.7 us
    pallas_call x1, Pallas kernels, expert(): pl.pallas_call(expert_kernel, grid=(2, steps), out_shape=(jax.ShapeDtypeS...  9.99 us
    unnamed x19, local copies, waits for them, and re-layouts  9.11 us

profile of v1, /device:TPU:6, one launch (start us, length us, event | category | flops | bytes accessed | tf_op | source)
XLA Modules:
  0.0 136.2 jit_solution(1408233495658298418)
XLA Ops:
  0.6 0.0 copy-start.1
  0.6 0.0 copy-start.2
  0.7 0.0 copy-start.3
  0.7 1.4 %fusion.4 = (s32[1]{0:T(128)}, s32[1]{0:T(128)}) fusion(s32[2]{0:T(128)} %param.8), kind=kLoop, calls=%fused_computation.21 | loop fusion | bytes 16 | tf_op jit(solution)/shard_map/slice | solution.py:359
  2.1 1.3 iota_compare_fusion
  3.4 1.0 constant_dynamic-update-slice_fusion.1
  4.3 1.0 constant_dynamic-update-slice_fusion
  5.3 1.1 select_select_fusion.send
  6.5 54.7 %dispatch.1 = (bf16[4,4,16,7168]{3,2,1,0:T(8,128)(2,1)}, bf16[2,8,224,128]{3,2,1,0:T(8,128)(2,1)}, bf16[2,8,224,128]{3,2,1,0:T(8,128)(2,1)}, bf16[8,16,3584]{2,1,0:T(8,128)(2,1)}) custom-call(bf16[4,16,7168]{2,1,0:T(8,128)(2,1)} %select_select_fusion.send, bf16[2,8,224,128]{3,2,1,0:T(8,128)(2,1)} %bitcast.43, bf16[2,8,224,128]{3,2,1,0:T(8,128)(2,1)} %bitcast.44, ...), custom_call_target="tpu_custom_call" | custom-call | tf_op jit(solution)/shard_map/dispatch/pallas_call | solution.py:141
  61.1 0.0 copy-done.1
  61.1 0.0 copy-done.2
  61.1 0.0 copy-done.3
  61.1 0.0 copy-start.4
  61.2 2.0 %copy-done.4 = bf16[4,4,16,7168]{3,2,1,0:T(8,128)(2,1)S(1)} copy-done((bf16[4,4,16,7168]{3,2,1,0:T(8,128)(2,1)S(1)}, bf16[4,4,16,7168]{3,2,1,0:T(8,128)(2,1)}, u32[]{:S(2)}) %copy-start.4) | copy-done | bytes 3670040
  63.2 0.0 copy-start.5
  63.2 1.2 copy-done.5
  64.4 1.2 copy-done.6
  65.5 1.2 copy-done.7
  66.7 10.0 %expert.1 = (bf16[256,3584]{1,0:T(8,128)(2,1)S(1)}, bf16[3,3584,256]{2,1,0:T(8,128)(2,1)}) custom-call(bf16[256,7168]{1,0:T(8,128)(2,1)S(1)} %bitcast.46, bf16[256,7168]{1,0:T(8,128)(2,1)S(1)} %bitcast.47, bf16[3584,128]{1,0:T(8,128)(2,1)S(1)} %copy-done.1, bf16[3584,128]{1,0:T(8,128)(2,1)S(1)} %bitcast.48, bf16[3584,128]{1,0:T(8,128)(2,1)S(1)} %copy-done.2, ...), custom_call_target="tpu_custom_call" | custom-call | flops 3758096384 | bytes 31457280 | tf_op jit(solution)/shard_map/expert/pallas_call | solution.py:202
  76.7 2.6 %copy-done = bf16[3,3584,256]{2,1,0:T(8,128)(2,1)S(1)} copy-done((bf16[3,3584,256]{2,1,0:T(8,128)(2,1)S(1)}, bf16[3,3584,256]{2,1,0:T(8,128)(2,1)}, u32[]{:S(2)}) %copy-start) | copy-done | bytes 5505048
  79.3 54.7 %combine.1 = (bf16[4,16,3584]{2,1,0:T(8,128)(2,1)S(1)}, f32[3,224,128]{2,1,0:T(8,128)S(1)}) custom-call(bf16[4,4,16,3584]{3,2,1,0:T(8,128)(2,1)S(1)} %bitcast.42, bf16[3,8,2,224,256]{4,3,2,1,0:T(8,128)(2,1)S(1)} %bitcast.41), custom_call_target="tpu_custom_call" | custom-call | tf_op jit(solution)/shard_map/combine/pallas_call | solution.py:324
  134.0 0.0 copy-done.8
  134.0 0.1 broadcast_in_dim.107
  134.1 0.1 broadcast_in_dim.108
  134.2 0.1 broadcast_in_dim.112
  134.3 0.1 broadcast_in_dim.113
  134.4 0.1 broadcast_in_dim.117
  134.4 0.1 broadcast_in_dim.118
  134.5 0.1 broadcast_in_dim.97
  134.6 0.1 broadcast_in_dim.98
  134.7 0.8 fusion.2
  135.5 0.7 slice_bitcast_fusion
  (7 shorter events, 0.1 us)
Async XLA Ops:
  0.6 60.5 %copy-start.1 = (bf16[3584,128]{1,0:T(8,128)(2,1)S(1)}, bf16[3584,128]{1,0:T(8,128)(2,1)}, u32[]{:S(2)}) copy-start(bf16[3584,128]{1,0:T(8,128)(2,1)} %wg.1) | copy-start | bytes 2752516
  0.6 60.5 %copy-start.2 = (bf16[3584,128]{1,0:T(8,128)(2,1)S(1)}, bf16[3584,128]{1,0:T(8,128)(2,1)}, u32[]{:S(2)}) copy-start(bf16[3584,128]{1,0:T(8,128)(2,1)} %wu.1) | copy-start | bytes 2752516
  0.7 60.5 %copy-start.3 = (bf16[128,3584]{1,0:T(8,128)(2,1)S(1)}, bf16[128,3584]{1,0:T(8,128)(2,1)}, u32[]{:S(2)}) copy-start(bf16[128,3584]{1,0:T(8,128)(2,1)} %wd.1) | copy-start | bytes 2752516
  61.1 2.0 %copy-start.4 = (bf16[4,4,16,7168]{3,2,1,0:T(8,128)(2,1)S(1)}, bf16[4,4,16,7168]{3,2,1,0:T(8,128)(2,1)}, u32[]{:S(2)}) copy-start(bf16[4,4,16,7168]{3,2,1,0:T(8,128)(2,1)} %get-tuple-element.12) | copy-start | bytes 11010052
  63.2 1.2 copy-start.5
  64.4 1.2 copy-start.6
  65.5 1.2 copy-start.7
  76.7 2.6 %copy-start = (bf16[3,3584,256]{2,1,0:T(8,128)(2,1)S(1)}, bf16[3,3584,256]{2,1,0:T(8,128)(2,1)}, u32[]{:S(2)}) copy-start(bf16[3,3584,256]{2,1,0:T(8,128)(2,1)} %get-tuple-element.17) | copy-start | bytes 16515076
  79.3 54.7 %copy-start.8 = (s32[2]{0:T(128)S(1)}, s32[2]{0:T(128)}, u32[]{:S(2)}) copy-start(s32[2]{0:T(128)} %param.8) | copy-start | bytes 28

commit v2 on v0

v2 whole, which is shorter than its diff:
```python
import functools
import math

import jax
import jax.numpy as jnp
from jax import lax
from jax.experimental import pallas as pl
from jax.experimental.pallas import tpu as pltpu
from jax.sharding import PartitionSpec as P

E_WIN = 4
NY = 8
NX = 4
BLK = 16
D = 3584
SLICE = 128
ROWS = 224
CHUNK = 896
N_ROWS = 256
MESH = pl.DeviceIdType.MESH
LEAN = (1, -1, 1, -1)
ORDER = (0, 1, 3, 2)


def place():
    ex = lax.axis_index("expert")
    rp = lax.axis_index("replica")
    z, y = lax.div(ex, NY), lax.rem(ex, NY)
    q, core = lax.div(rp, 2), lax.rem(rp, 2)
    x, zl = lax.div(q, 2), lax.rem(q, 2)

    def at_z(i):
        return (lax.rem(z + i, E_WIN) * NY + y, rp)

    def at_y(d):
        return (z * NY + lax.rem(y + NY + d, NY), rp)

    def at_x(i):
        return (ex, lax.rem(x + NX + i, NX) * 4 + zl * 2 + core)

    pair = (ex, x * 4 + (1 - zl) * 2 + core)
    sibling = (ex, q * 2 + 1 - core)
    return z, x, zl, q, core, at_z, at_y, at_x, pair, sibling


def remote(src, dst, send_sem, recv_sem, peer):
    return pltpu.make_async_remote_copy(
        src_ref=src, dst_ref=dst, send_sem=send_sem, recv_sem=recv_sem, device_id=peer, device_id_type=MESH
    )


def start(copies):
    for c in copies:
        c.start()


def slot(j, o):
    return pl.ds((ORDER.index(j) * 4 + o) * BLK, BLK)


def layer_kernel(scale, assign, tokens, cotangent, wg, wu, wd, ret, out,
                 send, rows, w, down, pre, dh, dcat, hid, px, dw, theirs, from_a, from_b, s2, from_z, s3, from_y, parts, sums,
                 ls, zs, zr, ys, yr, ws, wr, ps, pr, hs, hr, cs, cr, as_, ar, bs, br, gs, gr, fs, fr):
    f32, bf = jnp.float32, jnp.bfloat16
    by_cols = (((1,), (1,)), ((), ()))
    by_rows = (((0,), (0,)), ((), ()))
    z, x, zl, q, core, at_z, at_y, at_x, pair, sibling = place()

    peers = [at_z(i) for i in (1, 2, 3)] + [at_y(d) for d in (1, -1, 2, -2, 4)] + [at_x(i) for i in (1, 2, 3)] + [pair, sibling]
    barrier = pltpu.get_barrier_semaphore()
    for peer in peers:
        pl.semaphore_signal(barrier, inc=1, device_id=peer, device_id_type=MESH)

    keep = [
        pltpu.make_async_copy(wg, w.at[:, 0:SLICE], ls.at[0]),
        pltpu.make_async_copy(wu, w.at[:, 2 * SLICE : 3 * SLICE], ls.at[1]),
        pltpu.make_async_copy(wd, down.at[0:SLICE], ls.at[2]),
    ]
    start(keep)
    for c, src in enumerate((tokens, cotangent)):
        first, second = src[0:BLK], src[BLK : 2 * BLK]
        for e in range(E_WIN):
            other = jnp.where(assign[1] == e, second, jnp.zeros_like(second))
            send[c, e] = jnp.where(assign[0] == e, first, other)
        rows[c, slot(0, 0)] = send[c, z]
    pl.semaphore_wait(barrier, len(peers))

    half = pl.ds(pl.multiple_of(core * (D // 2), 128), D // 2)

    def weights(srcs, dsts, base, peer):
        return [remote(s, d, ws.at[base + n], wr.at[base + n], peer) for n, (s, d) in enumerate(zip(srcs, dsts))]

    def part(first, count):
        tall = pl.ds(pl.multiple_of(core * (D // 2) + first * ROWS, 32), count * ROWS)
        short = pl.ds(pl.multiple_of(SLICE + first * BLK, 16), count * BLK)
        return [w.at[tall, SLICE : 2 * SLICE], w.at[tall, 3 * SLICE : 4 * SLICE], down.at[short, half]]

    tall = pl.ds(pl.multiple_of(core * (D // 2) + q * ROWS, 32), ROWS)
    short = pl.ds(pl.multiple_of(q * BLK, 16), BLK)
    one, two, every = part(q, 1), part(2 * x, 2), part(0, 8)
    stage1 = weights([wg.at[tall], wu.at[tall], wd.at[short, half]], one, 0, at_y(4))
    stage2 = weights(one, one, 3, pair)
    stage3 = [weights(two, two, 6 + 3 * (i - 1), at_x(i)) for i in (1, 2, 3)]
    stage4 = weights(every, every, 15, sibling)

    by_z = {
        4 - i: [
            remote(send.at[c, lax.rem(z + i, E_WIN)], rows.at[c, slot(4 - i, 0)], zs.at[i - 1, c], zr.at[3 - i, c], at_z(i))
            for c in (0, 1)
        ]
        for i in (1, 2, 3)
    }

    def by_y(j, c):
        s = LEAN[j]
        return [
            remote(rows.at[c, slot(j, 0)], rows.at[c, slot(j, 1)], ys.at[j, 0, c], yr.at[j, 0, c], at_y(s)),
            remote(rows.at[c, slot(j, 0)], rows.at[c, slot(j, 2)], ys.at[j, 1, c], yr.at[j, 1, c], at_y(-s)),
            remote(rows.at[c, slot(j, 1)], rows.at[c, slot(j, 3)], ys.at[j, 2, c], yr.at[j, 2, c], at_y(s)),
        ]

    along_y = [[by_y(j, c) for c in (0, 1)] for j in range(E_WIN)]

    def spread(j):
        for c in (0, 1):
            if j:
                by_z[j][c].wait_recv()
            start(along_y[j][c][:2])

    def relay(j):
        for c in (0, 1):
            along_y[j][c][0].wait_recv()
            along_y[j][c][2].start()

    def landed(j):
        for c in (0, 1):
            along_y[j][c][1].wait_recv()
            along_y[j][c][2].wait_recv()

    def forward(lo, hi):
        pre[lo:hi] = jnp.zeros((hi - lo, 4 * SLICE), f32)
        dh[lo:hi] = jnp.zeros((hi - lo, 2 * SLICE), f32)

        @pl.loop(0, D // CHUNK)
        def _(n):
            cols = pl.ds(pl.multiple_of(n * CHUNK, 128), CHUNK)
            pre[lo:hi] += jnp.dot(rows[0, lo:hi, cols], w[cols, :], preferred_element_type=f32)
            dh[lo:hi] += lax.dot_general(rows[1, lo:hi, cols], down[:, cols], by_cols, preferred_element_type=f32)

    start(stage1)
    for c in (0, 1):
        by_z[3][c].start()
        by_z[1][c].start()
    spread(0)
    relay(0)
    start(by_z[2])
    for c in stage1:
        c.wait_recv()
    start(stage2)
    spread(1)
    spread(3)
    for c in stage2:
        c.wait_recv()
    for group in stage3:
        start(group)
    relay(1)
    relay(3)
    spread(2)
    for group in stage3:
        for c in group:
            c.wait_recv()
    start(stage4)
    relay(2)
    for c in keep:
        c.wait()
    for c in stage4:
        c.wait_recv()
    for j in ORDER[:3]:
        landed(j)
    forward(0, 3 * 64)
    landed(2)
    forward(3 * 64, N_ROWS)

    gate, up, grad = pre[:, : 2 * SLICE], pre[:, 2 * SLICE :], dh[...]
    sig = jax.nn.sigmoid(gate)
    silu = gate * sig
    hid[...] = (silu * up).astype(bf)
    dcat[:, 2 * SLICE :] = (grad * silu).astype(bf)
    dcat[:, : 2 * SLICE] = (grad * up * sig * (1.0 + gate * (1.0 - sig))).astype(bf)

    to_core = [remote(dw.at[k, :, 1 - core], theirs.at[k], cs.at[k], cr.at[k], sibling) for k in range(3)]
    ahead, beyond, behind = lax.rem(x + 1, NX), lax.rem(x + 2, NX), lax.rem(x + 3, NX)

    def grad_rows(k, target, n):
        return dw.at[k, 2 * target + n, core]

    by_a = [
        [
            remote(grad_rows(k, beyond, 0), from_a.at[k, 0], as_.at[k, 0], ar.at[k, 0], at_x(1)),
            remote(grad_rows(k, beyond, 1), from_a.at[k, 1], as_.at[k, 1], ar.at[k, 1], at_x(-1)),
        ]
        for k in range(3)
    ]
    by_b = [
        [
            remote(grad_rows(k, ahead, 1), from_b.at[k, 0, 1], bs.at[k, 0], br.at[k, 0], at_x(1)),
            remote(grad_rows(k, behind, 0), from_b.at[k, 1, 0], bs.at[k, 1], br.at[k, 1], at_x(-1)),
            remote(grad_rows(k, ahead, 0), from_b.at[k, 0, 0], bs.at[k, 2], br.at[k, 2], at_x(1)),
            remote(grad_rows(k, behind, 1), from_b.at[k, 1, 1], bs.at[k, 3], br.at[k, 3], at_x(-1)),
        ]
        for k in range(3)
    ]
    to_pair = [remote(s2.at[k, 1 - zl], from_z.at[k], gs.at[k], gr.at[k], pair) for k in range(3)]
    to_y = [remote(s3.at[k, 1], from_y.at[k], fs.at[k], fr.at[k], at_y(4)) for k in range(3)]

    def weight_grad(k):
        left = rows.at[k // 2]

        @pl.loop(0, D // CHUNK)
        def _(n):
            cols = pl.ds(pl.multiple_of(n * CHUNK, 128), CHUNK)
            right = hid[...] if k == 2 else dcat[:, 2 * SLICE * k : 2 * SLICE * (k + 1)]
            full = lax.dot_general(left[:, cols], right, by_rows, preferred_element_type=f32)
            dw[k, pl.ds(2 * n, 2)] = full.astype(bf).reshape(2, 2, ROWS, 2 * SLICE)

        to_core[k].start()

    def over_cores(k):
        to_core[k].wait_recv()

        @pl.loop(0, 8)
        def _(n):
            dw[k, n, core] = (dw[k, n, core].astype(f32) + theirs[k, n].astype(f32)).astype(bf)

        start(by_a[k])
        start(by_b[k][:2])

    def augment(k):
        for c, (target, n) in zip(by_a[k], ((ahead, 0), (behind, 1))):
            c.wait_recv()
            place_ = grad_rows(k, target, n)
            place_[...] = (place_[...].astype(f32) + from_a[k, n].astype(f32)).astype(bf)
        start(by_b[k][2:])

    def over_x(k):
        for c in by_b[k]:
            c.wait_recv()
        for n in (0, 1):
            total = dw[k, 2 * x + n, core].astype(f32) + from_b[k, 0, n].astype(f32) + from_b[k, 1, n].astype(f32)
            s2[k, n] = total.astype(bf)
        to_pair[k].start()

    def over_pair(k):
        to_pair[k].wait_recv()
        total = s2[k, zl].astype(f32) + from_z[k].astype(f32)
        s3[k, 0] = total[:, :SLICE].astype(bf)
        s3[k, 1] = total[:, SLICE:].astype(bf)
        to_y[k].start()

    def over_y(k):
        to_y[k].wait_recv()
        out[k] = (s3[k, 0].astype(f32) + from_y[k].astype(f32)) * scale

    back = [
        [
            remote(px.at[slot(j, o)], parts.at[j, o - 1], ps.at[j, o - 1], pr.at[j, o - 1], at_y(d * LEAN[j]))
            for o, d in ((1, -1), (2, 1), (3, -2))
        ]
        for j in range(E_WIN)
    ]
    home = {j: remote(sums.at[j], ret.at[z], hs.at[j - 1], hr.at[j - 1], at_z(j)) for j in (1, 2, 3)}
    landing = {j: remote(sums.at[j], ret.at[lax.rem(z + 4 - j, E_WIN)], hs.at[j - 1], hr.at[j - 1], at_z(j)) for j in (1, 2, 3)}
    stay = pltpu.make_async_copy(sums.at[0], ret.at[z], ls.at[3])

    def input_grad():
        @pl.loop(0, D // CHUNK)
        def _(n):
            cols = pl.ds(pl.multiple_of(n * CHUNK, 128), CHUNK)
            px[:, cols] = lax.dot_general(dcat[...], w[cols, :], by_cols, preferred_element_type=f32).astype(bf)

        for j in (2, 1, 3, 0):
            start(back[j][::-1])

    def gather(j):
        for c in back[j]:
            c.wait_recv()
        total = px[slot(j, 0)].astype(f32)
        for o in range(3):
            total += parts[j, o].astype(f32)
        sums[j] = total.astype(bf)
        if j:
            home[j].start()
        else:
            stay.start()

    weight_grad(0)
    input_grad()
    weight_grad(1)
    over_cores(0)
    weight_grad(2)
    over_cores(1)
    over_cores(2)
    augment(0)
    gather(2)
    augment(1)
    gather(1)
    augment(2)
    over_x(0)
    gather(3)
    over_pair(0)
    over_x(1)
    gather(0)
    over_pair(1)
    over_y(0)
    over_x(2)
    over_pair(2)
    over_y(1)
    over_y(2)

    stay.wait()
    for j in (1, 2, 3):
        landing[j].wait_recv()
        home[j].wait_send()
    groups = list(by_z.values()) + [g for both in along_y for g in both] + stage3 + [stage1, stage2, stage4]
    for group in groups + back + by_a + by_b + [to_core, to_pair, to_y]:
        for c in group:
            c.wait_send()


def layer(assign, tokens, cotangent, wg, wu, wd, scale):
    f32, bf = jnp.float32, jnp.bfloat16
    dma = pltpu.SemaphoreType.DMA
    anywhere = pl.BlockSpec(memory_space=pl.ANY)
    vmem = pl.BlockSpec(memory_space=pltpu.VMEM)
    return pl.pallas_call(
        functools.partial(layer_kernel, scale),
        out_shape=(
            jax.ShapeDtypeStruct((E_WIN, BLK, D), bf),
            jax.ShapeDtypeStruct((3, ROWS, SLICE), f32),
        ),
        in_specs=[pl.BlockSpec(memory_space=pltpu.SMEM), vmem, vmem, anywhere, anywhere, anywhere],
        out_specs=(anywhere, vmem),
        scratch_shapes=[
            pltpu.VMEM((2, E_WIN, BLK, D), bf),
            pltpu.VMEM((2, N_ROWS, D), bf),
            pltpu.VMEM((D, 4 * SLICE), bf),
            pltpu.VMEM((2 * SLICE, D), bf),
            pltpu.VMEM((N_ROWS, 4 * SLICE), f32),
            pltpu.VMEM((N_ROWS, 2 * SLICE), f32),
            pltpu.VMEM((N_ROWS, 4 * SLICE), bf),
            pltpu.VMEM((N_ROWS, 2 * SLICE), bf),
            pltpu.VMEM((N_ROWS, D), bf),
            pltpu.VMEM((3, 8, 2, ROWS, 2 * SLICE), bf),
            pltpu.VMEM((3, 8, ROWS, 2 * SLICE), bf),
            pltpu.VMEM((3, 2, ROWS, 2 * SLICE), bf),
            pltpu.VMEM((3, 2, 2, ROWS, 2 * SLICE), bf),
            pltpu.VMEM((3, 2, ROWS, 2 * SLICE), bf),
            pltpu.VMEM((3, ROWS, 2 * SLICE), bf),
            pltpu.VMEM((3, 2, ROWS, SLICE), bf),
            pltpu.VMEM((3, ROWS, SLICE), bf),
            pltpu.VMEM((E_WIN, 3, BLK, D), bf),
            pltpu.VMEM((E_WIN, BLK, D), bf),
            dma((4,)),
            dma((3, 2)), dma((3, 2)),
            dma((4, 3, 2)), dma((4, 3, 2)),
            dma((18,)), dma((18,)),
            dma((4, 3)), dma((4, 3)),
            dma((3,)), dma((3,)),
            dma((3,)), dma((3,)),
            dma((3, 2)), dma((3, 2)),
            dma((3, 4)), dma((3, 4)),
            dma((3,)), dma((3,)),
            dma((3,)), dma((3,)),
        ],
        compiler_params=pltpu.CompilerParams(collective_id=0, has_side_effects=True, vmem_limit_bytes=56 * 2**20),
        cost_estimate=pl.CostEstimate(flops=16 * N_ROWS * D * 2 * SLICE, bytes_accessed=2**24, transcendentals=0),
        name="layer",
    )(assign, tokens, cotangent, wg, wu, wd)


def shards(tokens, cotangent, assign, w_gate, w_up, w_down):
    scale = 1.0 / math.sqrt(lax.axis_size("expert") * lax.axis_size("replica") * BLK // 2)
    ret, grads = layer(assign, tokens, cotangent, w_gate, w_up, w_down, scale)
    picked = jnp.zeros((2, BLK, D), jnp.bfloat16)
    for e in range(E_WIN):
        picked = jnp.where((assign == e)[:, None, None], ret[e], picked)
    return picked.reshape(2 * BLK, D), grads[0], grads[1], jnp.transpose(grads[2])


def solution(mesh):
    placed = (
        P(("expert", "replica"), None),
        P(("expert", "replica"), None),
        P(("expert", "replica")),
        P(None, "expert"),
        P(None, "expert"),
        P("expert", None),
    )
    return jax.shard_map(
        shards,
        mesh=mesh,
        in_specs=placed,
        out_specs=(
            P(("expert", "replica"), None),
            P("replica", "expert"),
            P("replica", "expert"),
            P("expert", "replica"),
        ),
        check_vma=False,
    )
```

time: 542 us -> 119 us (0.22); the launches traced: 535 us -> 118 us
  waiting for transfers between devices: 351 us -> 0 us
  Pallas kernels: 0 us -> 113 us
  blocking collectives: 103 us -> 0 us
  starting transfers between devices: 29.2 us -> 0 us
  matrix products: 24.1 us -> 0 us
  between operations: 13.9 us -> 0.66 us
  other arithmetic: 9.14 us -> 0.81 us
    reduce_scatter x3 -> x0, waiting for transfers between devices: 247 us -> none  [the longest x1 97.7 us: backprop(): lax.psum_scatter(grad_down.astype(jnp.bfloat16), 'replica', scatter_dimen...]
    pallas_call x0 -> x1, Pallas kernels: none -> 113 us  [layer(): pl.pallas_call(functools.partial(layer_kernel, scale), out_shape=(jax.Sha...]
    all_to_all x2 -> x0, waiting for transfers between devices: 103 us -> none  [the longest x1 103 us: shards(): lax.all_to_all(send_dy, 'expert', split_axis=0, concat_axis=0, tiled=True)]
    all_to_all x1 -> x0, blocking collectives: 103 us -> none  [shards(): lax.all_to_all(send_x, 'expert', split_axis=0, concat_axis=0, tiled=True)]
    all_to_all x2 -> x0, starting transfers between devices: 29.1 us -> none  [the longest x1 18.9 us: shards(): lax.all_to_all(result_back, 'expert', split_axis=0, concat_axis=0, tiled=...]
    dot_general x8 -> x0, matrix products: 24.1 us -> none  [the longest x1 4.19 us: backprop(): lax.dot_general(flat_dy, hidden, by_rows, preferred_element_type=jnp.floa...]
  transfers between devices with their start and end apart: 5 -> 0, of which waited for: 4 -> 0; matrix products, arithmetic and copies ran while one was open for 4% -> 0% of each run, Pallas kernels for 0% -> 0%
where the time goes in v2:
time: 119 us; the launch traced here: 118 us
  Pallas kernels  113 us (95%)
  local copies, waits for them, and re-layouts  3.29 us (3%)
    pallas_call x1, Pallas kernels, layer(): pl.pallas_call(functools.partial(layer_kernel, scale), out_shape=(jax.Sha...  113 us

profile of v2, /device:TPU:6, one launch (start us, length us, event | category | flops | bytes accessed | tf_op | source)
XLA Modules:
  0.0 117.9 jit_solution(6343641434689923870)
XLA Ops:
  0.6 113.1 %layer.1 = (bf16[4,16,3584]{2,1,0:T(8,128)(2,1)}, f32[3,224,128]{2,1,0:T(8,128)}) custom-call(s32[2]{0:T(128)} %assign.1, bf16[32,3584]{1,0:T(8,128)(2,1)} %tokens.1, bf16[32,3584]{1,0:T(8,128)(2,1)} %cotangent.1, bf16[3584,128]{1,0:T(8,128)(2,1)} %wg.1, bf16[3584,128]{1,0:T(8,128)(2,1)} %wu.1, bf16[128,3584]{1,0:T(8,128)(2,1)} %wd.1), custom_call_target="tpu_custom_call" | custom-call | flops 3758096384 | bytes 16777216 | tf_op jit(solution)/shard_map/layer/pallas_call | solution.py:335
  113.7 1.1 slice_bitcast_fusion.6
  114.8 0.0 copy-start.1
  114.9 0.6 copy-done.1
  115.5 0.1 broadcast_in_dim.67
  115.6 0.1 broadcast_in_dim.68
  115.7 0.1 broadcast_in_dim.72
  115.7 0.1 broadcast_in_dim.73
  115.8 0.1 broadcast_in_dim.77
  115.9 0.1 broadcast_in_dim.78
  116.0 0.1 broadcast_in_dim.82
  116.1 0.1 broadcast_in_dim.83
  116.2 0.0 copy-start
  116.2 0.8 fusion.2
  117.0 0.2 copy-done
  117.1 0.7 slice_bitcast_fusion
  (1 shorter events, 0.0 us)
Async XLA Ops:
  114.8 0.7 copy-start.1
  116.2 1.0 copy-start

commit v3 on v2

v3 whole, which is shorter than its diff:
```python
import functools
import math

import jax
import jax.numpy as jnp
from jax import lax
from jax.experimental import pallas as pl
from jax.experimental.pallas import tpu as pltpu
from jax.sharding import PartitionSpec as P

E_WIN = 4
NY = 8
NX = 4
BLK = 16
D = 3584
SLICE = 128
ROWS = 224
CHUNK = 896
N_ROWS = 256
MESH = pl.DeviceIdType.MESH
LEAN = (1, -1, 1, -1)
ORDER = (0, 1, 3, 2)


def place():
    ex = lax.axis_index("expert")
    rp = lax.axis_index("replica")
    z, y = lax.div(ex, NY), lax.rem(ex, NY)
    q, core = lax.div(rp, 2), lax.rem(rp, 2)
    x, zl = lax.div(q, 2), lax.rem(q, 2)

    def at_z(i):
        return (lax.rem(z + i, E_WIN) * NY + y, rp)

    def at_y(d):
        return (z * NY + lax.rem(y + NY + d, NY), rp)

    def at_x(i):
        return (ex, lax.rem(x + NX + i, NX) * 4 + zl * 2 + core)

    pair = (ex, x * 4 + (1 - zl) * 2 + core)
    sibling = (ex, q * 2 + 1 - core)
    return z, x, zl, q, core, at_z, at_y, at_x, pair, sibling


def remote(src, dst, send_sem, recv_sem, peer):
    return pltpu.make_async_remote_copy(
        src_ref=src, dst_ref=dst, send_sem=send_sem, recv_sem=recv_sem, device_id=peer, device_id_type=MESH
    )


def start(copies):
    for c in copies:
        c.start()


def slot(j, o):
    return pl.ds((ORDER.index(j) * 4 + o) * BLK, BLK)


def layer_kernel(scale, assign, tokens, cotangent, wg, wu, wd, grad_in, out_gate, out_up, out_down,
                 own, send, rows, w, down, pre, dh, dcat, hid, px, dw, theirs, from_pair, from_a, from_b, s2, from_z, s3, from_y,
                 parts, sums, ret,
                 ls, zs, zr, ys, yr, ws, wr, ps, pr, hs, hr, cs, cr, as_, ar, bs, br, gs, gr, fs, fr):
    f32, bf = jnp.float32, jnp.bfloat16
    by_cols = (((1,), (1,)), ((), ()))
    by_rows = (((0,), (0,)), ((), ()))
    z, x, zl, q, core, at_z, at_y, at_x, pair, sibling = place()

    peers = [at_z(i) for i in (1, 2, 3)] + [at_y(d) for d in (1, -1, 2, -2, 4)] + [at_x(i) for i in (1, 2, 3)] + [pair, sibling]
    barrier = pltpu.get_barrier_semaphore()
    for peer in peers:
        pl.semaphore_signal(barrier, inc=1, device_id=peer, device_id_type=MESH)

    bring = [pltpu.make_async_copy(src, own.at[c], ls.at[3 + c]) for c, src in enumerate((tokens, cotangent))]
    start(bring)
    keep = [
        pltpu.make_async_copy(wg, w.at[:, 0:SLICE], ls.at[0]),
        pltpu.make_async_copy(wu, w.at[:, SLICE : 2 * SLICE], ls.at[1]),
        pltpu.make_async_copy(wd, down.at[0:SLICE], ls.at[2]),
    ]
    for c in (0, 1):
        bring[c].wait()
        first, second = own[c, 0:BLK], own[c, BLK : 2 * BLK]
        for e in range(E_WIN):
            other = jnp.where(assign[1] == e, second, jnp.zeros_like(second))
            send[c, e] = jnp.where(assign[0] == e, first, other)
        rows[c, slot(0, 0)] = send[c, z]
    pl.semaphore_wait(barrier, len(peers))

    half = pl.ds(pl.multiple_of(core * (D // 2), 128), D // 2)

    def weights(srcs, dsts, base, peer):
        return [remote(s, d, ws.at[base + n], wr.at[base + n], peer) for n, (s, d) in enumerate(zip(srcs, dsts))]

    def part(first, count):
        tall = pl.ds(pl.multiple_of(core * (D // 2) + first * ROWS, 32), count * ROWS)
        short = pl.ds(pl.multiple_of(SLICE + first * BLK, 16), count * BLK)
        return [w.at[tall, 2 * SLICE : 3 * SLICE], w.at[tall, 3 * SLICE : 4 * SLICE], down.at[short, half]]

    tall = pl.ds(pl.multiple_of(core * (D // 2) + q * ROWS, 32), ROWS)
    short = pl.ds(pl.multiple_of(q * BLK, 16), BLK)
    one, two, every = part(q, 1), part(2 * x, 2), part(0, 8)
    stage1 = weights([wg.at[tall], wu.at[tall], wd.at[short, half]], one, 0, at_y(4))
    stage2 = weights(one, one, 3, pair)
    stage3 = [weights(two, two, 6 + 3 * (i - 1), at_x(i)) for i in (1, 2, 3)]
    stage4 = weights(every, every, 15, sibling)

    by_z = {
        4 - i: [
            remote(send.at[c, lax.rem(z + i, E_WIN)], rows.at[c, slot(4 - i, 0)], zs.at[i - 1, c], zr.at[3 - i, c], at_z(i))
            for c in (0, 1)
        ]
        for i in (1, 2, 3)
    }

    def by_y(j, c):
        s = LEAN[j]
        return [
            remote(rows.at[c, slot(j, 0)], rows.at[c, slot(j, 1)], ys.at[j, 0, c], yr.at[j, 0, c], at_y(s)),
            remote(rows.at[c, slot(j, 0)], rows.at[c, slot(j, 2)], ys.at[j, 1, c], yr.at[j, 1, c], at_y(-s)),
            remote(rows.at[c, slot(j, 1)], rows.at[c, slot(j, 3)], ys.at[j, 2, c], yr.at[j, 2, c], at_y(s)),
        ]

    along_y = [[by_y(j, c) for c in (0, 1)] for j in range(E_WIN)]

    def spread(j, c):
        if j:
            by_z[j][c].wait_recv()
        start(along_y[j][c][:2])

    def relay(j, c):
        along_y[j][c][0].wait_recv()
        along_y[j][c][2].start()

    def landed(j):
        for c in (0, 1):
            along_y[j][c][1].wait_recv()
            along_y[j][c][2].wait_recv()

    def arrived(stage):
        for c in stage:
            c.wait_recv()

    def forward(lo, hi):
        pre[lo:hi] = jnp.zeros((hi - lo, 4 * SLICE), f32)
        dh[lo:hi] = jnp.zeros((hi - lo, 2 * SLICE), f32)

        @pl.loop(0, D // CHUNK)
        def _(n):
            cols = pl.ds(pl.multiple_of(n * CHUNK, 128), CHUNK)
            pre[lo:hi] += jnp.dot(rows[0, lo:hi, cols], w[cols, :], preferred_element_type=f32)
            dh[lo:hi] += lax.dot_general(rows[1, lo:hi, cols], down[:, cols], by_cols, preferred_element_type=f32)

    start(stage1)
    for c in (0, 1):
        by_z[3][c].start()
        by_z[1][c].start()
        spread(0, c)
    start(keep)
    relay(0, 0)
    start(by_z[2])
    spread(1, 0)
    spread(3, 0)
    relay(0, 1)
    spread(1, 1)
    spread(3, 1)
    arrived(stage1)
    start(stage2)
    relay(1, 0)
    relay(3, 0)
    arrived(stage2)
    for group in stage3:
        start(group)
    relay(1, 1)
    relay(3, 1)
    spread(2, 0)
    spread(2, 1)
    relay(2, 0)
    relay(2, 1)
    for group in stage3:
        arrived(group)
    start(stage4)
    for c in keep:
        c.wait()
    arrived(stage4)
    for j in ORDER[:3]:
        landed(j)
    forward(0, 3 * 64)
    landed(2)
    forward(3 * 64, N_ROWS)

    for h in (0, 1):
        a, b, c = 2 * h * SLICE, (2 * h + 1) * SLICE, (2 * h + 2) * SLICE
        gate, up, grad = pre[:, a:b], pre[:, b:c], dh[:, h * SLICE : (h + 1) * SLICE]
        sig = jax.nn.sigmoid(gate)
        silu = gate * sig
        hid[:, h * SLICE : (h + 1) * SLICE] = (silu * up).astype(bf)
        dcat[:, b:c] = (grad * silu).astype(bf)
        dcat[:, a:b] = (grad * up * sig * (1.0 + gate * (1.0 - sig))).astype(bf)

    near = {off: lax.rem(x + off, NX) for off in range(NX)}
    NEAR = (2, 1, 3, 0)
    LOW = ROWS // 2

    to_core = [
        {off: remote(dw.at[k, n, :, 1 - core], theirs.at[k, n], cs.at[k, off], cr.at[k, off], sibling) for off, n in near.items()}
        for k in range(3)
    ]
    first_pair = {off: remote(dw.at[0, n, 1 - zl, core], from_pair.at[n], gs.at[off], gr.at[off], pair) for off, n in near.items()}

    def piece(k, off, t):
        n = near[off]
        return dw.at[k, n, t, core] if k else dw.at[0, n, zl, core, LOW * t : LOW * (t + 1)]

    def in_a(k, t):
        return from_a.at[k, t] if k else from_a.at[0, t, 0:LOW]

    def in_b(k, side, t):
        return from_b.at[k, side, t] if k else from_b.at[0, side, t, 0:LOW]

    by_a = [
        [
            remote(piece(k, 2, 0), in_a(k, 0), as_.at[k, 0], ar.at[k, 0], at_x(1)),
            remote(piece(k, 2, 1), in_a(k, 1), as_.at[k, 1], ar.at[k, 1], at_x(-1)),
        ]
        for k in range(3)
    ]
    by_b = [
        [
            remote(piece(k, 1, 1), in_b(k, 0, 1), bs.at[k, 0], br.at[k, 0], at_x(1)),
            remote(piece(k, 3, 0), in_b(k, 1, 0), bs.at[k, 1], br.at[k, 1], at_x(-1)),
            remote(piece(k, 1, 0), in_b(k, 0, 0), bs.at[k, 2], br.at[k, 2], at_x(1)),
            remote(piece(k, 3, 1), in_b(k, 1, 1), bs.at[k, 3], br.at[k, 3], at_x(-1)),
        ]
        for k in range(3)
    ]
    to_pair = {k: remote(s2.at[k - 1, 1 - zl], from_z.at[k - 1], gs.at[3 + k], gr.at[3 + k], pair) for k in (1, 2)}
    to_y = {
        1: remote(s3.at[0], from_y.at[0:2], fs.at[0], fr.at[0], at_y(4)),
        2: remote(s3.at[1, 1], from_y.at[2], fs.at[1], fr.at[1], at_y(4)),
    }

    def weight_grad(k):
        for off in NEAR:
            n = near[off]
            cols = pl.ds(pl.multiple_of(n * CHUNK, 128), CHUNK)
            right = hid[...] if k == 2 else dcat[:, 2 * SLICE * k : 2 * SLICE * (k + 1)]
            full = lax.dot_general(rows[k // 2, :, cols], right, by_rows, preferred_element_type=f32)
            dw[k, n] = full.astype(bf).reshape(2, 2, ROWS, 2 * SLICE)
            to_core[k][off].start()

    def leave_x(k, off):
        if off == 2:
            start(by_a[k])
        elif off:
            by_b[k][off // 2].start()

    def over_cores(k):
        for off in NEAR:
            n = near[off]
            to_core[k][off].wait_recv()
            for t in (0, 1):
                dw[k, n, t, core] = (dw[k, n, t, core].astype(f32) + theirs[k, n, t].astype(f32)).astype(bf)
            if k:
                leave_x(k, off)
            else:
                first_pair[off].start()

    def over_pair_first():
        for off in NEAR:
            n = near[off]
            first_pair[off].wait_recv()
            dw[0, n, zl, core] = (dw[0, n, zl, core].astype(f32) + from_pair[n].astype(f32)).astype(bf)
            leave_x(0, off)

    def augment(k):
        for t, off in ((0, 1), (1, 3)):
            by_a[k][t].wait_recv()
            spot = piece(k, off, t)
            spot[...] = (spot[...].astype(f32) + in_a(k, t)[...].astype(f32)).astype(bf)
            by_b[k][2 + t].start()

    def x_total(k, t):
        return piece(k, 0, t)[...].astype(f32) + in_b(k, 0, t)[...].astype(f32) + in_b(k, 1, t)[...].astype(f32)

    def over_x(k):
        for c in by_b[k]:
            c.wait_recv()
        if k:
            s2[k - 1, 1 - zl] = x_total(k, 1 - zl).astype(bf)
            to_pair[k].start()
            s2[k - 1, zl] = x_total(k, zl).astype(bf)
        else:
            for t in (0, 1):
                total = x_total(0, t) * scale
                out_gate[LOW * t : LOW * (t + 1)] = total[:, :SLICE]
                out_up[LOW * t : LOW * (t + 1)] = total[:, SLICE:]

    def over_pair(k):
        to_pair[k].wait_recv()
        total = s2[k - 1, zl].astype(f32) + from_z[k - 1].astype(f32)
        s3[k - 1, 0] = total[:, :SLICE].astype(bf)
        s3[k - 1, 1] = total[:, SLICE:].astype(bf)
        to_y[k].start()

    def over_y(k):
        to_y[k].wait_recv()
        if k == 1:
            out_gate[...] += from_y[0].astype(f32) * scale
            out_up[...] += from_y[1].astype(f32) * scale
        else:
            out_down[...] = (s3[1, 0].astype(f32) + from_y[2].astype(f32)) * scale

    back = [
        [
            remote(px.at[slot(j, o)], parts.at[j, o - 1], ps.at[j, o - 1], pr.at[j, o - 1], at_y(d * LEAN[j]))
            for o, d in ((1, -1), (2, 1), (3, -2))
        ]
        for j in range(E_WIN)
    ]
    home = {j: remote(sums.at[j], ret.at[z], hs.at[j - 1], hr.at[j - 1], at_z(j)) for j in (1, 2, 3)}
    landing = {j: remote(sums.at[j], ret.at[lax.rem(z + 4 - j, E_WIN)], hs.at[j - 1], hr.at[j - 1], at_z(j)) for j in (1, 2, 3)}

    def input_grad():
        @pl.loop(0, D // CHUNK)
        def _(n):
            cols = pl.ds(pl.multiple_of(n * CHUNK, 128), CHUNK)
            px[:, cols] = lax.dot_general(dcat[...], w[cols, :], by_cols, preferred_element_type=f32).astype(bf)

        for j in (2, 1, 3, 0):
            start(back[j][::-1])

    def gather(j):
        arrived(back[j])
        total = px[slot(j, 0)].astype(f32)
        for o in range(3):
            total += parts[j, o].astype(f32)
        if j:
            sums[j] = total.astype(bf)
            home[j].start()
        else:
            ret[z] = total.astype(bf)

    weight_grad(1)
    weight_grad(0)
    over_cores(1)
    input_grad()
    over_cores(0)
    weight_grad(2)
    augment(1)
    over_cores(2)
    over_x(1)
    augment(2)
    over_pair_first()
    over_pair(1)
    augment(0)
    gather(2)
    over_x(2)
    gather(1)
    gather(3)
    over_pair(2)
    gather(0)
    over_x(0)
    over_y(1)
    over_y(2)

    for j in (1, 2, 3):
        landing[j].wait_recv()
    for b in (0, 1):
        mine = ret[0]
        for e in range(1, E_WIN):
            mine = jnp.where(assign[b] == e, ret[e], mine)
        grad_in[b * BLK : (b + 1) * BLK] = mine

    groups = list(by_z.values()) + [g for both in along_y for g in both] + stage3 + [stage1, stage2, stage4]
    groups += back + by_a + by_b + [list(g.values()) for g in to_core + [first_pair, to_pair, to_y, home]]
    for group in groups:
        for c in group:
            c.wait_send()


def layer(assign, tokens, cotangent, wg, wu, wd, scale):
    f32, bf = jnp.float32, jnp.bfloat16
    dma = pltpu.SemaphoreType.DMA
    anywhere = pl.BlockSpec(memory_space=pl.ANY)
    vmem = pl.BlockSpec(memory_space=pltpu.VMEM)
    return pl.pallas_call(
        functools.partial(layer_kernel, scale),
        out_shape=(
            jax.ShapeDtypeStruct((2 * BLK, D), bf),
            jax.ShapeDtypeStruct((ROWS, SLICE), f32),
            jax.ShapeDtypeStruct((ROWS, SLICE), f32),
            jax.ShapeDtypeStruct((ROWS, SLICE), f32),
        ),
        in_specs=[pl.BlockSpec(memory_space=pltpu.SMEM)] + [anywhere] * 5,
        out_specs=(vmem, vmem, vmem, vmem),
        scratch_shapes=[
            pltpu.VMEM((2, 2 * BLK, D), bf),
            pltpu.VMEM((2, E_WIN, BLK, D), bf),
            pltpu.VMEM((2, N_ROWS, D), bf),
            pltpu.VMEM((D, 4 * SLICE), bf),
            pltpu.VMEM((2 * SLICE, D), bf),
            pltpu.VMEM((N_ROWS, 4 * SLICE), f32),
            pltpu.VMEM((N_ROWS, 2 * SLICE), f32),
            pltpu.VMEM((N_ROWS, 4 * SLICE), bf),
            pltpu.VMEM((N_ROWS, 2 * SLICE), bf),
            pltpu.VMEM((N_ROWS, D), bf),
            pltpu.VMEM((3, NX, 2, 2, ROWS, 2 * SLICE), bf),
            pltpu.VMEM((3, NX, 2, ROWS, 2 * SLICE), bf),
            pltpu.VMEM((NX, ROWS, 2 * SLICE), bf),
            pltpu.VMEM((3, 2, ROWS, 2 * SLICE), bf),
            pltpu.VMEM((3, 2, 2, ROWS, 2 * SLICE), bf),
            pltpu.VMEM((2, 2, ROWS, 2 * SLICE), bf),
            pltpu.VMEM((2, ROWS, 2 * SLICE), bf),
            pltpu.VMEM((2, 2, ROWS, SLICE), bf),
            pltpu.VMEM((3, ROWS, SLICE), bf),
            pltpu.VMEM((E_WIN, 3, BLK, D), bf),
            pltpu.VMEM((E_WIN, BLK, D), bf),
            pltpu.VMEM((E_WIN, BLK, D), bf),
            dma((5,)),
            dma((3, 2)), dma((3, 2)),
            dma((4, 3, 2)), dma((4, 3, 2)),
            dma((18,)), dma((18,)),
            dma((4, 3)), dma((4, 3)),
            dma((3,)), dma((3,)),
            dma((3, 4)), dma((3, 4)),
            dma((3, 2)), dma((3, 2)),
            dma((3, 4)), dma((3, 4)),
            dma((6,)), dma((6,)),
            dma((2,)), dma((2,)),
        ],
        compiler_params=pltpu.CompilerParams(collective_id=0, has_side_effects=True, vmem_limit_bytes=56 * 2**20),
        cost_estimate=pl.CostEstimate(flops=16 * N_ROWS * D * 2 * SLICE, bytes_accessed=2**24, transcendentals=0),
        name="layer",
    )(assign, tokens, cotangent, wg, wu, wd)


def shards(tokens, cotangent, assign, w_gate, w_up, w_down):
    scale = 1.0 / math.sqrt(lax.axis_size("expert") * lax.axis_size("replica") * BLK // 2)
    grad_in, gate, up, down = layer(assign, tokens, cotangent, w_gate, w_up, w_down, scale)
    return grad_in, gate, up, jnp.transpose(down)


def solution(mesh):
    placed = (
        P(("expert", "replica"), None),
        P(("expert", "replica"), None),
        P(("expert", "replica")),
        P(None, "expert"),
        P(None, "expert"),
        P("expert", None),
    )
    return jax.shard_map(
        shards,
        mesh=mesh,
        in_specs=placed,
        out_specs=(
            P(("expert", "replica"), None),
            P("replica", "expert"),
            P("replica", "expert"),
            P("expert", "replica"),
        ),
        check_vma=False,
    )
```

time: 119 us -> 111 us (0.933)
  Pallas kernels: 113 us -> 106 us
    pallas_call x1, Pallas kernels: 113 us -> 106 us  [layer(): pl.pallas_call(functools.partial(layer_kernel, scale), out_shape=(jax.Sha...]
    unnamed x4 -> x10, local copies, waits for them, and re-layouts: 0.82 us -> 4.2 us
where the time goes in v3:
time: 111 us
  Pallas kernels  106 us (95%)
  local copies, waits for them, and re-layouts  4.2 us (4%)
    pallas_call x1, Pallas kernels, layer(): pl.pallas_call(functools.partial(layer_kernel, scale), out_shape=(jax.Sha...  106 us
    unnamed x10, local copies, waits for them, and re-layouts  4.2 us

profile of v3, /device:TPU:6, one launch (start us, length us, event | category | flops | bytes accessed | tf_op | source)
XLA Modules:
  0.0 110.9 jit_solution(7313070967950178587)
XLA Ops:
  0.6 106.0 %layer.1 = (bf16[32,3584]{1,0:T(8,128)(2,1)}, f32[224,128]{1,0:T(8,128)}, f32[224,128]{1,0:T(8,128)}, f32[224,128]{1,0:T(8,128)}) custom-call(s32[2]{0:T(128)} %assign.1, bf16[32,3584]{1,0:T(8,128)(2,1)} %tokens.1, bf16[32,3584]{1,0:T(8,128)(2,1)} %cotangent.1, bf16[3584,128]{1,0:T(8,128)(2,1)} %wg.1, bf16[3584,128]{1,0:T(8,128)(2,1)} %wu.1, ...), custom_call_target="tpu_custom_call" | custom-call | flops 3758096384 | bytes 16777216 | tf_op jit(solution)/shard_map/layer/pallas_call | solution.py:388
  106.6 0.0 copy-start.2
  106.7 1.7 %copy.14 = bf16[32,3584]{1,0:T(8,128)(2,1)} copy(bf16[32,3584]{1,0:T(8,128)(2,1)} %get-tuple-element.16) | data formatting | bytes 458752
  108.3 0.0 copy-done.2
  108.3 0.0 copy-start.1
  108.3 0.6 copy.15
  109.0 0.3 copy-done.1
  109.3 0.0 copy-start
  109.3 0.6 copy.16
  109.9 0.3 copy-done
  110.2 0.6 copy.17
Async XLA Ops:
  106.6 1.7 %copy-start.2 = (f32[224,128]{1,0:T(8,128)S(1)}, f32[224,128]{1,0:T(8,128)}, u32[]{:S(2)}) copy-start(f32[224,128]{1,0:T(8,128)} %get-tuple-element.17) | copy-start | bytes 344068
  108.3 0.9 copy-start.1
  109.3 0.9 copy-start

commit v4 on v3

--- a/solution.py
+++ b/solution.py
@@ -40,7 +40,8 @@
 
     pair = (ex, x * 4 + (1 - zl) * 2 + core)
     sibling = (ex, q * 2 + 1 - core)
-    return z, x, zl, q, core, at_z, at_y, at_x, pair, sibling
+    diagonal = (at_y(4)[0], pair[1])
+    return z, x, zl, q, core, at_z, at_y, at_x, pair, sibling, diagonal
 
 
 def remote(src, dst, send_sem, recv_sem, peer):
@@ -60,14 +61,14 @@
 
 def layer_kernel(scale, assign, tokens, cotangent, wg, wu, wd, grad_in, out_gate, out_up, out_down,
                  own, send, rows, w, down, pre, dh, dcat, hid, px, dw, theirs, from_pair, from_a, from_b, s2, from_z, s3, from_y,
-                 parts, sums, ret,
+                 s2d, from_d, mid, parts, sums, ret,
                  ls, zs, zr, ys, yr, ws, wr, ps, pr, hs, hr, cs, cr, as_, ar, bs, br, gs, gr, fs, fr):
     f32, bf = jnp.float32, jnp.bfloat16
     by_cols = (((1,), (1,)), ((), ()))
     by_rows = (((0,), (0,)), ((), ()))
-    z, x, zl, q, core, at_z, at_y, at_x, pair, sibling = place()
-
-    peers = [at_z(i) for i in (1, 2, 3)] + [at_y(d) for d in (1, -1, 2, -2, 4)] + [at_x(i) for i in (1, 2, 3)] + [pair, sibling]
+    z, x, zl, q, core, at_z, at_y, at_x, pair, sibling, diagonal = place()
+
+    peers = [at_z(i) for i in (1, 2, 3)] + [at_y(d) for d in (1, -1, 4)] + [at_x(i) for i in (1, 2, 3)] + [pair, sibling, diagonal]
     barrier = pltpu.get_barrier_semaphore()
     for peer in peers:
         pl.semaphore_signal(barrier, inc=1, device_id=peer, device_id_type=MESH)
@@ -79,13 +80,14 @@
         pltpu.make_async_copy(wu, w.at[:, SLICE : 2 * SLICE], ls.at[1]),
         pltpu.make_async_copy(wd, down.at[0:SLICE], ls.at[2]),
     ]
-    for c in (0, 1):
+    def select(c):
         bring[c].wait()
         first, second = own[c, 0:BLK], own[c, BLK : 2 * BLK]
         for e in range(E_WIN):
             other = jnp.where(assign[1] == e, second, jnp.zeros_like(second))
             send[c, e] = jnp.where(assign[0] == e, first, other)
         rows[c, slot(0, 0)] = send[c, z]
+
     pl.semaphore_wait(barrier, len(peers))
 
     half = pl.ds(pl.multiple_of(core * (D // 2), 128), D // 2)
@@ -152,35 +154,50 @@
             pre[lo:hi] += jnp.dot(rows[0, lo:hi, cols], w[cols, :], preferred_element_type=f32)
             dh[lo:hi] += lax.dot_general(rows[1, lo:hi, cols], down[:, cols], by_cols, preferred_element_type=f32)
 
+    def pass_on(stage, n):
+        if stage == 1:
+            stage1[n].wait_recv()
+            stage2[n].start()
+        elif stage == 2:
+            stage2[n].wait_recv()
+            for group in stage3:
+                group[n].start()
+        else:
+            for group in stage3:
+                group[n].wait_recv()
+            stage4[n].start()
+
     start(stage1)
     for c in (0, 1):
+        select(c)
         by_z[3][c].start()
         by_z[1][c].start()
         spread(0, c)
     start(keep)
+    pass_on(1, 0)
     relay(0, 0)
     start(by_z[2])
+    pass_on(2, 0)
+    pass_on(1, 1)
     spread(1, 0)
     spread(3, 0)
     relay(0, 1)
+    pass_on(2, 1)
+    pass_on(1, 2)
     spread(1, 1)
     spread(3, 1)
-    arrived(stage1)
-    start(stage2)
+    pass_on(2, 2)
     relay(1, 0)
     relay(3, 0)
-    arrived(stage2)
-    for group in stage3:
-        start(group)
+    pass_on(3, 0)
     relay(1, 1)
     relay(3, 1)
     spread(2, 0)
+    pass_on(3, 1)
     spread(2, 1)
     relay(2, 0)
+    pass_on(3, 2)
     relay(2, 1)
-    for group in stage3:
-        arrived(group)
-    start(stage4)
     for c in keep:
         c.wait()
     arrived(stage4)
@@ -235,11 +252,13 @@
         ]
         for k in range(3)
     ]
-    to_pair = {k: remote(s2.at[k - 1, 1 - zl], from_z.at[k - 1], gs.at[3 + k], gr.at[3 + k], pair) for k in (1, 2)}
-    to_y = {
-        1: remote(s3.at[0], from_y.at[0:2], fs.at[0], fr.at[0], at_y(4)),
-        2: remote(s3.at[1, 1], from_y.at[2], fs.at[1], fr.at[1], at_y(4)),
-    }
+    to_pair = remote(s2.at[0, 1 - zl], from_z, gs.at[4], gr.at[4], pair)
+    to_y = remote(s3, from_y, fs.at[0], fr.at[0], at_y(4))
+    spread_down = [
+        remote(s2d.at[1 - zl, 1], from_d.at[2], fs.at[3], fr.at[3], diagonal),
+        remote(s2d.at[zl, 1], from_d.at[1], fs.at[2], fr.at[2], at_y(4)),
+        remote(s2d.at[1 - zl, 0], from_d.at[0], fs.at[1], fr.at[1], pair),
+    ]
 
     def weight_grad(k):
         for off in NEAR:
@@ -287,38 +306,46 @@
     def over_x(k):
         for c in by_b[k]:
             c.wait_recv()
-        if k:
-            s2[k - 1, 1 - zl] = x_total(k, 1 - zl).astype(bf)
-            to_pair[k].start()
-            s2[k - 1, zl] = x_total(k, zl).astype(bf)
+        if k == 1:
+            s2[0, 1 - zl] = x_total(1, 1 - zl).astype(bf)
+            to_pair.start()
+            s2[0, zl] = x_total(1, zl).astype(bf)
+        elif k == 2:
+            for t in (1 - zl, zl):
+                total = x_total(2, t).astype(bf)
+                s2d[t, 0] = total[:, :SLICE]
+                s2d[t, 1] = total[:, SLICE:]
+            start(spread_down)
         else:
             for t in (0, 1):
                 total = x_total(0, t) * scale
                 out_gate[LOW * t : LOW * (t + 1)] = total[:, :SLICE]
                 out_up[LOW * t : LOW * (t + 1)] = total[:, SLICE:]
 
-    def over_pair(k):
-        to_pair[k].wait_recv()
-        total = s2[k - 1, zl].astype(f32) + from_z[k - 1].astype(f32)
-        s3[k - 1, 0] = total[:, :SLICE].astype(bf)
-        s3[k - 1, 1] = total[:, SLICE:].astype(bf)
-        to_y[k].start()
-
-    def over_y(k):
-        to_y[k].wait_recv()
-        if k == 1:
-            out_gate[...] += from_y[0].astype(f32) * scale
-            out_up[...] += from_y[1].astype(f32) * scale
-        else:
-            out_down[...] = (s3[1, 0].astype(f32) + from_y[2].astype(f32)) * scale
-
-    back = [
-        [
-            remote(px.at[slot(j, o)], parts.at[j, o - 1], ps.at[j, o - 1], pr.at[j, o - 1], at_y(d * LEAN[j]))
-            for o, d in ((1, -1), (2, 1), (3, -2))
+    def over_pair():
+        to_pair.wait_recv()
+        s3[...] = (s2[0, zl].astype(f32) + from_z[...].astype(f32)).astype(bf)
+        to_y.start()
+
+    def finish():
+        to_y.wait_recv()
+        out_gate[...] += from_y[:, :SLICE].astype(f32) * scale
+        out_up[...] += from_y[:, SLICE:].astype(f32) * scale
+        arrived(spread_down)
+        total = s2d[zl, 0].astype(f32)
+        for n in range(3):
+            total += from_d[n].astype(f32)
+        out_down[...] = total * scale
+
+    def backward(j):
+        s = LEAN[j]
+        return [
+            remote(px.at[slot(j, 3)], mid.at[j], ps.at[j, 0], pr.at[j, 0], at_y(-s)),
+            remote(px.at[slot(j, 2)], parts.at[j, 1], ps.at[j, 1], pr.at[j, 1], at_y(s)),
+            remote(px.at[slot(j, 1)], parts.at[j, 0], ps.at[j, 2], pr.at[j, 2], at_y(-s)),
         ]
-        for j in range(E_WIN)
-    ]
+
+    back = [backward(j) for j in range(E_WIN)]
     home = {j: remote(sums.at[j], ret.at[z], hs.at[j - 1], hr.at[j - 1], at_z(j)) for j in (1, 2, 3)}
     landing = {j: remote(sums.at[j], ret.at[lax.rem(z + 4 - j, E_WIN)], hs.at[j - 1], hr.at[j - 1], at_z(j)) for j in (1, 2, 3)}
 
@@ -329,13 +356,17 @@
             px[:, cols] = lax.dot_general(dcat[...], w[cols, :], by_cols, preferred_element_type=f32).astype(bf)
 
         for j in (2, 1, 3, 0):
-            start(back[j][::-1])
+            start(back[j][:2])
+
+    def meet(j):
+        back[j][0].wait_recv()
+        spot = slot(j, 1)
+        px[spot] = (px[spot].astype(f32) + mid[j].astype(f32)).astype(bf)
+        back[j][2].start()
 
     def gather(j):
-        arrived(back[j])
-        total = px[slot(j, 0)].astype(f32)
-        for o in range(3):
-            total += parts[j, o].astype(f32)
+        arrived(back[j][1:])
+        total = px[slot(j, 0)].astype(f32) + parts[j, 0].astype(f32) + parts[j, 1].astype(f32)
         if j:
             sums[j] = total.astype(bf)
             home[j].start()
@@ -350,20 +381,20 @@
     weight_grad(2)
     augment(1)
     over_cores(2)
+    for j in (2, 1, 3, 0):
+        meet(j)
     over_x(1)
     augment(2)
+    over_pair()
     over_pair_first()
-    over_pair(1)
-    augment(0)
     gather(2)
     over_x(2)
+    augment(0)
     gather(1)
     gather(3)
-    over_pair(2)
     gather(0)
     over_x(0)
-    over_y(1)
-    over_y(2)
+    finish()
 
     for j in (1, 2, 3):
         landing[j].wait_recv()
@@ -374,7 +405,7 @@
         grad_in[b * BLK : (b + 1) * BLK] = mine
 
     groups = list(by_z.values()) + [g for both in along_y for g in both] + stage3 + [stage1, stage2, stage4]
-    groups += back + by_a + by_b + [list(g.values()) for g in to_core + [first_pair, to_pair, to_y, home]]
+    groups += back + by_a + by_b + [[to_pair, to_y], spread_down] + [list(g.values()) for g in to_core + [first_pair, home]]
     for group in groups:
         for c in group:
             c.wait_send()
@@ -411,11 +442,14 @@
             pltpu.VMEM((NX, ROWS, 2 * SLICE), bf),
             pltpu.VMEM((3, 2, ROWS, 2 * SLICE), bf),
             pltpu.VMEM((3, 2, 2, ROWS, 2 * SLICE), bf),
-            pltpu.VMEM((2, 2, ROWS, 2 * SLICE), bf),
-            pltpu.VMEM((2, ROWS, 2 * SLICE), bf),
+            pltpu.VMEM((1, 2, ROWS, 2 * SLICE), bf),
+            pltpu.VMEM((ROWS, 2 * SLICE), bf),
+            pltpu.VMEM((ROWS, 2 * SLICE), bf),
+            pltpu.VMEM((ROWS, 2 * SLICE), bf),
             pltpu.VMEM((2, 2, ROWS, SLICE), bf),
             pltpu.VMEM((3, ROWS, SLICE), bf),
-            pltpu.VMEM((E_WIN, 3, BLK, D), bf),
+            pltpu.VMEM((E_WIN, BLK, D), bf),
+            pltpu.VMEM((E_WIN, 2, BLK, D), bf),
             pltpu.VMEM((E_WIN, BLK, D), bf),
             pltpu.VMEM((E_WIN, BLK, D), bf),
             dma((5,)),
@@ -427,8 +461,8 @@
             dma((3, 4)), dma((3, 4)),
             dma((3, 2)), dma((3, 2)),
             dma((3, 4)), dma((3, 4)),
-            dma((6,)), dma((6,)),
-            dma((2,)), dma((2,)),
+            dma((5,)), dma((5,)),
+            dma((4,)), dma((4,)),
         ],
         compiler_params=pltpu.CompilerParams(collective_id=0, has_side_effects=True, vmem_limit_bytes=56 * 2**20),
         cost_estimate=pl.CostEstimate(flops=16 * N_ROWS * D * 2 * SLICE, bytes_accessed=2**24, transcendentals=0),
@@ -436,9 +470,29 @@
     )(assign, tokens, cotangent, wg, wu, wd)
 
 
+def hand_over_kernel(*refs):
+    sems = refs[-1]
+    copies = [pltpu.make_async_copy(refs[n], refs[4 + n], sems.at[n]) for n in range(4)]
+    start(copies)
+    for c in copies:
+        c.wait()
+
+
+def hand_over(*arrays):
+    hbm = pl.BlockSpec(memory_space=pltpu.HBM)
+    return pl.pallas_call(
+        hand_over_kernel,
+        out_shape=tuple(jax.ShapeDtypeStruct(a.shape, a.dtype) for a in arrays),
+        in_specs=[hbm] * 4,
+        out_specs=[hbm] * 4,
+        scratch_shapes=[pltpu.SemaphoreType.DMA((4,))],
+        name="hand_over",
+    )(*arrays)
+
+
 def shards(tokens, cotangent, assign, w_gate, w_up, w_down):
     scale = 1.0 / math.sqrt(lax.axis_size("expert") * lax.axis_size("replica") * BLK // 2)
-    grad_in, gate, up, down = layer(assign, tokens, cotangent, w_gate, w_up, w_down, scale)
+    grad_in, gate, up, down = hand_over(*layer(assign, tokens, cotangent, w_gate, w_up, w_down, scale))
     return grad_in, gate, up, jnp.transpose(down)
 
 

time: 111 us -> 119 us (1.072)
  Pallas kernels: 106 us -> 118 us
  local copies, waits for them, and re-layouts: 4.2 us -> 0 us
    pallas_call x0 -> x1, Pallas kernels: none -> 18.5 us  [hand_over(): pl.pallas_call(hand_over_kernel, out_shape=tuple((jax.ShapeDtypeStruct(a....]
    pallas_call x1, Pallas kernels: 106 us -> 99.5 us  [layer(): pl.pallas_call(functools.partial(layer_kernel, scale), out_shape=(jax.Sha...]
    unnamed x10 -> x0, local copies, waits for them, and re-layouts: 4.2 us -> none
where the time goes in v4:
time: 119 us
  Pallas kernels  118 us (99%)
    pallas_call x1, Pallas kernels, layer(): pl.pallas_call(functools.partial(layer_kernel, scale), out_shape=(jax.Sha...  99.5 us
    pallas_call x1, Pallas kernels, hand_over(): pl.pallas_call(hand_over_kernel, out_shape=tuple((jax.ShapeDtypeStruct(a....  18.5 us

profile of v4, /device:TPU:6, one launch (start us, length us, event | category | flops | bytes accessed | tf_op | source)
XLA Modules:
  0.0 118.6 jit_solution(62168954498695063)
XLA Ops:
  0.6 99.5 %layer.1 = (bf16[32,3584]{1,0:T(8,128)(2,1)}, f32[224,128]{1,0:T(8,128)}, f32[224,128]{1,0:T(8,128)}, f32[224,128]{1,0:T(8,128)}) custom-call(s32[2]{0:T(128)} %assign.1, bf16[32,3584]{1,0:T(8,128)(2,1)} %tokens.1, bf16[32,3584]{1,0:T(8,128)(2,1)} %cotangent.1, bf16[3584,128]{1,0:T(8,128)(2,1)} %wg.1, bf16[3584,128]{1,0:T(8,128)(2,1)} %wu.1, ...), custom_call_target="tpu_custom_call" | custom-call | flops 3758096384 | bytes 16777216 | tf_op jit(solution)/shard_map/layer/pallas_call | solution.py:419
  100.1 18.5 %hand_over.1 = (bf16[32,3584]{1,0:T(8,128)(2,1)}, f32[224,128]{1,0:T(8,128)}, f32[224,128]{1,0:T(8,128)}, f32[224,128]{1,0:T(8,128)}) custom-call(bf16[32,3584]{1,0:T(8,128)(2,1)} %get-tuple-element.12.refs_0_, f32[224,128]{1,0:T(8,128)} %get-tuple-element.13.refs_1_, f32[224,128]{1,0:T(8,128)} %get-tuple-element.14.refs_2_, ...), custom_call_target="tpu_custom_call" | custom-call | tf_op jit(solution)/shard_map/hand_over/pallas_call | solution.py:483

commit v5 on v4

--- a/solution.py
+++ b/solution.py
@@ -18,7 +18,7 @@
 CHUNK = 896
 N_ROWS = 256
 MESH = pl.DeviceIdType.MESH
-LEAN = (1, -1, 1, -1)
+LEAN = (1, -1, -1, 1)
 ORDER = (0, 1, 3, 2)
 
 
@@ -88,8 +88,6 @@
             send[c, e] = jnp.where(assign[0] == e, first, other)
         rows[c, slot(0, 0)] = send[c, z]
 
-    pl.semaphore_wait(barrier, len(peers))
-
     half = pl.ds(pl.multiple_of(core * (D // 2), 128), D // 2)
 
     def weights(srcs, dsts, base, peer):
@@ -167,21 +165,26 @@
                 group[n].wait_recv()
             stage4[n].start()
 
+    pl.semaphore_wait(barrier, len(peers))
     start(stage1)
-    for c in (0, 1):
-        select(c)
-        by_z[3][c].start()
-        by_z[1][c].start()
-        spread(0, c)
+    select(0)
+    by_z[3][0].start()
+    by_z[1][0].start()
+    spread(0, 0)
+    select(1)
+    by_z[3][1].start()
+    by_z[1][1].start()
+    spread(0, 1)
     start(keep)
     pass_on(1, 0)
     relay(0, 0)
-    start(by_z[2])
     pass_on(2, 0)
     pass_on(1, 1)
+    relay(0, 1)
+    by_z[2][0].start()
+    by_z[2][1].start()
     spread(1, 0)
     spread(3, 0)
-    relay(0, 1)
     pass_on(2, 1)
     pass_on(1, 2)
     spread(1, 1)
@@ -272,8 +275,11 @@
     def leave_x(k, off):
         if off == 2:
             start(by_a[k])
-        elif off:
+        elif off and k == 0:
             by_b[k][off // 2].start()
+
+    def rest(k):
+        start(by_b[k][:2])
 
     def over_cores(k):
         for off in NEAR:
@@ -355,8 +361,8 @@
             cols = pl.ds(pl.multiple_of(n * CHUNK, 128), CHUNK)
             px[:, cols] = lax.dot_general(dcat[...], w[cols, :], by_cols, preferred_element_type=f32).astype(bf)
 
-        for j in (2, 1, 3, 0):
-            start(back[j][:2])
+    def leave(j):
+        start(back[j][:2])
 
     def meet(j):
         back[j][0].wait_recv()
@@ -373,24 +379,32 @@
         else:
             ret[z] = total.astype(bf)
 
+    input_grad()
+    leave(2)
     weight_grad(1)
+    leave(1)
     weight_grad(0)
+    leave(3)
     over_cores(1)
-    input_grad()
+    rest(1)
+    leave(0)
     over_cores(0)
+    meet(2)
     weight_grad(2)
     augment(1)
+    meet(1)
     over_cores(2)
-    for j in (2, 1, 3, 0):
-        meet(j)
+    rest(2)
+    meet(3)
+    augment(2)
+    meet(0)
     over_x(1)
-    augment(2)
+    gather(2)
+    over_pair_first()
     over_pair()
-    over_pair_first()
-    gather(2)
+    gather(1)
     over_x(2)
     augment(0)
-    gather(1)
     gather(3)
     gather(0)
     over_x(0)
@@ -471,21 +485,17 @@
 
 
 def hand_over_kernel(*refs):
-    sems = refs[-1]
-    copies = [pltpu.make_async_copy(refs[n], refs[4 + n], sems.at[n]) for n in range(4)]
-    start(copies)
-    for c in copies:
-        c.wait()
+    for n in range(4):
+        refs[4 + n][...] = refs[n][...]
 
 
 def hand_over(*arrays):
-    hbm = pl.BlockSpec(memory_space=pltpu.HBM)
+    vmem = pl.BlockSpec(memory_space=pltpu.VMEM)
     return pl.pallas_call(
         hand_over_kernel,
         out_shape=tuple(jax.ShapeDtypeStruct(a.shape, a.dtype) for a in arrays),
-        in_specs=[hbm] * 4,
-        out_specs=[hbm] * 4,
-        scratch_shapes=[pltpu.SemaphoreType.DMA((4,))],
+        in_specs=[vmem] * 4,
+        out_specs=[vmem] * 4,
         name="hand_over",
     )(*arrays)
 

time: 119 us -> 99.3 us (0.83); the launches traced: 119 us -> 97.7 us
  Pallas kernels: 118 us -> 97.1 us
    pallas_call x1, Pallas kernels: 18.5 us -> 1.93 us  [hand_over(): pl.pallas_call(hand_over_kernel, out_shape=tuple((jax.ShapeDtypeStruct(a....]
    pallas_call x1, Pallas kernels: 99.5 us -> 95.2 us  [layer(): pl.pallas_call(functools.partial(layer_kernel, scale), out_shape=(jax.Sha...]
where the time goes in v5:
time: 99.3 us; the launch traced here: 97.7 us
  Pallas kernels  97.1 us (98%)
    pallas_call x1, Pallas kernels, layer(): pl.pallas_call(functools.partial(layer_kernel, scale), out_shape=(jax.Sha...  95.2 us

profile of v5, /device:TPU:6, one launch (start us, length us, event | category | flops | bytes accessed | tf_op | source)
XLA Modules:
  0.0 97.7 jit_solution(9330953512964837345)
XLA Ops:
  0.6 95.2 %layer.1 = (bf16[32,3584]{1,0:T(8,128)(2,1)}, f32[224,128]{1,0:T(8,128)}, f32[224,128]{1,0:T(8,128)}, f32[224,128]{1,0:T(8,128)}) custom-call(s32[2]{0:T(128)} %assign.1, bf16[32,3584]{1,0:T(8,128)(2,1)} %tokens.1, bf16[32,3584]{1,0:T(8,128)(2,1)} %cotangent.1, bf16[3584,128]{1,0:T(8,128)(2,1)} %wg.1, bf16[3584,128]{1,0:T(8,128)(2,1)} %wu.1, ...), custom_call_target="tpu_custom_call" | custom-call | flops 3758096384 | bytes 16777216 | tf_op jit(solution)/shard_map/layer/pallas_call | solution.py:433
  95.8 1.9 %hand_over.1 = (bf16[32,3584]{1,0:T(8,128)(2,1)}, f32[224,128]{1,0:T(8,128)}, f32[224,128]{1,0:T(8,128)}, f32[224,128]{1,0:T(8,128)}) custom-call(bf16[32,3584]{1,0:T(8,128)(2,1)} %get-tuple-element.12.refs_0_, f32[224,128]{1,0:T(8,128)} %get-tuple-element.13.refs_1_, f32[224,128]{1,0:T(8,128)} %get-tuple-element.14.refs_2_, ...), custom_call_target="tpu_custom_call" | custom-call | tf_op jit(solution)/shard_map/hand_over/pallas_call | solution.py:494

commit v6 on v5

--- a/solution.py
+++ b/solution.py
@@ -223,11 +223,8 @@
     NEAR = (2, 1, 3, 0)
     LOW = ROWS // 2
 
-    to_core = [
-        {off: remote(dw.at[k, n, :, 1 - core], theirs.at[k, n], cs.at[k, off], cr.at[k, off], sibling) for off, n in near.items()}
-        for k in range(3)
-    ]
-    first_pair = {off: remote(dw.at[0, n, 1 - zl, core], from_pair.at[n], gs.at[off], gr.at[off], pair) for off, n in near.items()}
+    to_core = [remote(dw.at[k, :, :, 1 - core], theirs.at[k], cs.at[k], cr.at[k], sibling) for k in range(3)]
+    first_pair = remote(dw.at[0, :, 1 - zl, core], from_pair, gs.at[0], gr.at[0], pair)
 
     def piece(k, off, t):
         n = near[off]
@@ -270,7 +267,7 @@
             right = hid[...] if k == 2 else dcat[:, 2 * SLICE * k : 2 * SLICE * (k + 1)]
             full = lax.dot_general(rows[k // 2, :, cols], right, by_rows, preferred_element_type=f32)
             dw[k, n] = full.astype(bf).reshape(2, 2, ROWS, 2 * SLICE)
-            to_core[k][off].start()
+        to_core[k].start()
 
     def leave_x(k, off):
         if off == 2:
@@ -282,20 +279,20 @@
         start(by_b[k][:2])
 
     def over_cores(k):
+        to_core[k].wait_recv()
         for off in NEAR:
             n = near[off]
-            to_core[k][off].wait_recv()
             for t in (0, 1):
                 dw[k, n, t, core] = (dw[k, n, t, core].astype(f32) + theirs[k, n, t].astype(f32)).astype(bf)
             if k:
                 leave_x(k, off)
-            else:
-                first_pair[off].start()
+        if k == 0:
+            first_pair.start()
 
     def over_pair_first():
+        first_pair.wait_recv()
         for off in NEAR:
             n = near[off]
-            first_pair[off].wait_recv()
             dw[0, n, zl, core] = (dw[0, n, zl, core].astype(f32) + from_pair[n].astype(f32)).astype(bf)
             leave_x(0, off)
 
@@ -379,29 +376,29 @@
         else:
             ret[z] = total.astype(bf)
 
+    weight_grad(1)
+    weight_grad(0)
     input_grad()
     leave(2)
-    weight_grad(1)
-    leave(1)
-    weight_grad(0)
-    leave(3)
     over_cores(1)
     rest(1)
+    leave(1)
+    over_cores(0)
+    leave(3)
+    weight_grad(2)
     leave(0)
-    over_cores(0)
+    augment(1)
     meet(2)
-    weight_grad(2)
-    augment(1)
-    meet(1)
     over_cores(2)
     rest(2)
+    meet(1)
     meet(3)
     augment(2)
     meet(0)
     over_x(1)
     gather(2)
+    over_pair()
     over_pair_first()
-    over_pair()
     gather(1)
     over_x(2)
     augment(0)
@@ -419,7 +416,7 @@
         grad_in[b * BLK : (b + 1) * BLK] = mine
 
     groups = list(by_z.values()) + [g for both in along_y for g in both] + stage3 + [stage1, stage2, stage4]
-    groups += back + by_a + by_b + [[to_pair, to_y], spread_down] + [list(g.values()) for g in to_core + [first_pair, home]]
+    groups += back + by_a + by_b + [[to_pair, to_y, first_pair], to_core, spread_down, list(home.values())]
     for group in groups:
         for c in group:
             c.wait_send()
@@ -472,7 +469,7 @@
             dma((18,)), dma((18,)),
             dma((4, 3)), dma((4, 3)),
             dma((3,)), dma((3,)),
-            dma((3, 4)), dma((3, 4)),
+            dma((3,)), dma((3,)),
             dma((3, 2)), dma((3, 2)),
             dma((3, 4)), dma((3, 4)),
             dma((5,)), dma((5,)),

time: 99.3 us -> 97.2 us (0.979)
  Pallas kernels: 97.1 us -> 95.6 us
    pallas_call x1, Pallas kernels: 95.2 us -> 93.7 us  [layer(): pl.pallas_call(functools.partial(layer_kernel, scale), out_shape=(jax.Sha...]
where the time goes in v6:
time: 97.2 us; the launch traced here: 96.2 us
  Pallas kernels  95.6 us (98%)
    pallas_call x1, Pallas kernels, layer(): pl.pallas_call(functools.partial(layer_kernel, scale), out_shape=(jax.Sha...  93.7 us

profile of v6, /device:TPU:6, one launch (start us, length us, event | category | flops | bytes accessed | tf_op | source)
XLA Modules:
  0.0 96.2 jit_solution(1676273267500698748)
XLA Ops:
  0.6 93.7 %layer.1 = (bf16[32,3584]{1,0:T(8,128)(2,1)}, f32[224,128]{1,0:T(8,128)}, f32[224,128]{1,0:T(8,128)}, f32[224,128]{1,0:T(8,128)}) custom-call(s32[2]{0:T(128)} %assign.1, bf16[32,3584]{1,0:T(8,128)(2,1)} %tokens.1, bf16[32,3584]{1,0:T(8,128)(2,1)} %cotangent.1, bf16[3584,128]{1,0:T(8,128)(2,1)} %wg.1, bf16[3584,128]{1,0:T(8,128)(2,1)} %wu.1, ...), custom_call_target="tpu_custom_call" | custom-call | flops 3758096384 | bytes 16777216 | tf_op jit(solution)/shard_map/layer/pallas_call | solution.py:430
  94.3 1.9 %hand_over.1 = (bf16[32,3584]{1,0:T(8,128)(2,1)}, f32[224,128]{1,0:T(8,128)}, f32[224,128]{1,0:T(8,128)}, f32[224,128]{1,0:T(8,128)}) custom-call(bf16[32,3584]{1,0:T(8,128)(2,1)} %get-tuple-element.12.refs_0_, f32[224,128]{1,0:T(8,128)} %get-tuple-element.13.refs_1_, f32[224,128]{1,0:T(8,128)} %get-tuple-element.14.refs_2_, ...), custom_call_target="tpu_custom_call" | custom-call | tf_op jit(solution)/shard_map/hand_over/pallas_call | solution.py:491

commit v7 on v6

--- a/solution.py
+++ b/solution.py
@@ -378,6 +378,7 @@
 
     weight_grad(1)
     weight_grad(0)
+    weight_grad(2)
     input_grad()
     leave(2)
     over_cores(1)
@@ -385,7 +386,6 @@
     leave(1)
     over_cores(0)
     leave(3)
-    weight_grad(2)
     leave(0)
     augment(1)
     meet(2)

time: 97.2 us -> 100 us (1.029)
  Pallas kernels: 95.6 us -> 99.1 us
    pallas_call x1, Pallas kernels: 93.7 us -> 97.1 us  [layer(): pl.pallas_call(functools.partial(layer_kernel, scale), out_shape=(jax.Sha...]
where the time goes in v7:
time: 100 us; the launch traced here: 99.7 us
  Pallas kernels  99.1 us (99%)
    pallas_call x1, Pallas kernels, layer(): pl.pallas_call(functools.partial(layer_kernel, scale), out_shape=(jax.Sha...  97.1 us

profile of v7, /device:TPU:6, one launch (start us, length us, event | category | flops | bytes accessed | tf_op | source)
XLA Modules:
  0.0 99.7 jit_solution(5751219521225610908)
XLA Ops:
  0.6 97.1 %layer.1 = (bf16[32,3584]{1,0:T(8,128)(2,1)}, f32[224,128]{1,0:T(8,128)}, f32[224,128]{1,0:T(8,128)}, f32[224,128]{1,0:T(8,128)}) custom-call(s32[2]{0:T(128)} %assign.1, bf16[32,3584]{1,0:T(8,128)(2,1)} %tokens.1, bf16[32,3584]{1,0:T(8,128)(2,1)} %cotangent.1, bf16[3584,128]{1,0:T(8,128)(2,1)} %wg.1, bf16[3584,128]{1,0:T(8,128)(2,1)} %wu.1, ...), custom_call_target="tpu_custom_call" | custom-call | flops 3758096384 | bytes 16777216 | tf_op jit(solution)/shard_map/layer/pallas_call | solution.py:430
  97.8 1.9 %hand_over.1 = (bf16[32,3584]{1,0:T(8,128)(2,1)}, f32[224,128]{1,0:T(8,128)}, f32[224,128]{1,0:T(8,128)}, f32[224,128]{1,0:T(8,128)}) custom-call(bf16[32,3584]{1,0:T(8,128)(2,1)} %get-tuple-element.12.refs_0_, f32[224,128]{1,0:T(8,128)} %get-tuple-element.13.refs_1_, f32[224,128]{1,0:T(8,128)} %get-tuple-element.14.refs_2_, ...), custom_call_target="tpu_custom_call" | custom-call | tf_op jit(solution)/shard_map/hand_over/pallas_call | solution.py:491

commit v8 on v6

--- a/solution.py
+++ b/solution.py
@@ -378,10 +378,10 @@
 
     weight_grad(1)
     weight_grad(0)
+    over_cores(1)
+    rest(1)
     input_grad()
     leave(2)
-    over_cores(1)
-    rest(1)
     leave(1)
     over_cores(0)
     leave(3)

time: 97.2 us -> 99 us (1.019)
  Pallas kernels: 95.6 us -> 96.9 us
    pallas_call x1, Pallas kernels: 93.7 us -> 95 us  [layer(): pl.pallas_call(functools.partial(layer_kernel, scale), out_shape=(jax.Sha...]
where the time goes in v8:
time: 99 us; the launch traced here: 97.6 us
  Pallas kernels  96.9 us (98%)
    pallas_call x1, Pallas kernels, layer(): pl.pallas_call(functools.partial(layer_kernel, scale), out_shape=(jax.Sha...  95 us

profile of v8, /device:TPU:6, one launch (start us, length us, event | category | flops | bytes accessed | tf_op | source)
XLA Modules:
  0.0 97.6 jit_solution(15205584941317725465)
XLA Ops:
  0.6 95.0 %layer.1 = (bf16[32,3584]{1,0:T(8,128)(2,1)}, f32[224,128]{1,0:T(8,128)}, f32[224,128]{1,0:T(8,128)}, f32[224,128]{1,0:T(8,128)}) custom-call(s32[2]{0:T(128)} %assign.1, bf16[32,3584]{1,0:T(8,128)(2,1)} %tokens.1, bf16[32,3584]{1,0:T(8,128)(2,1)} %cotangent.1, bf16[3584,128]{1,0:T(8,128)(2,1)} %wg.1, bf16[3584,128]{1,0:T(8,128)(2,1)} %wu.1, ...), custom_call_target="tpu_custom_call" | custom-call | flops 3758096384 | bytes 16777216 | tf_op jit(solution)/shard_map/layer/pallas_call | solution.py:430
  95.6 1.9 %hand_over.1 = (bf16[32,3584]{1,0:T(8,128)(2,1)}, f32[224,128]{1,0:T(8,128)}, f32[224,128]{1,0:T(8,128)}, f32[224,128]{1,0:T(8,128)}) custom-call(bf16[32,3584]{1,0:T(8,128)(2,1)} %get-tuple-element.12.refs_0_, f32[224,128]{1,0:T(8,128)} %get-tuple-element.13.refs_1_, f32[224,128]{1,0:T(8,128)} %get-tuple-element.14.refs_2_, ...), custom_call_target="tpu_custom_call" | custom-call | tf_op jit(solution)/shard_map/hand_over/pallas_call | solution.py:491
